TPU v7x, 512 devices: a whole 4x8x8 slice. The times are simulated.
512 devices in a mesh: user: 32 (over y_hi, z), item: 16 (over y_lo, x, core).
Axes of the slice: x: 4, y: 8 (y_hi: 4, y_lo: 2; y = y_hi * 2 + y_lo), z: 8, core: 2. Of those that a mesh axis runs over, the one named last changes fastest.
Arguments:
- user_table: bfloat16 [32768, 256], P('user'), may hold values from -2.5 to 2.5
- item_table: bfloat16 [16384, 256], P('item'), may hold values from -2.5 to 2.5
- user_ids: int32 [16384], P('user'), may hold values from 0 to 1023
- item_ids: int32 [4096], P('item'), may hold values from 0 to 1023
- user_drop: int32 [16384], P('user'), may hold values 0 or 1
- item_drop: int32 [4096], P('item'), may hold values 0 or 1
- user_content: bfloat16 [16384, 2048], P('user', 'item'), may hold values from -256 to 256
- item_content: bfloat16 [4096, 2048], P('item', 'user'), may hold values from -256 to 256
- user_pref_w: bfloat16 [256, 1024], P(None, 'item'), may hold values from -0.125 to 0.125
- user_content_w: bfloat16 [2048, 1024], P(None, 'item'), may hold values from -0.125 to 0.125
- user_gain: float32 [1024], P('item'), may hold values from 0.1 to 1.9
- user_shift: float32 [1024], P('item'), may hold values from -2.5 to 2.5
- item_pref_w: bfloat16 [256, 1024], P(None, 'user'), may hold values from -0.125 to 0.125
- item_content_w: bfloat16 [2048, 1024], P(None, 'user'), may hold values from -0.125 to 0.125
- item_gain: float32 [1024], P('user'), may hold values from 0.1 to 1.9
- item_shift: float32 [1024], P('user'), may hold values from -2.5 to 2.5
Outputs:
- grad_user_pref_w: float32 [256, 1024], P('user', 'item')
- grad_user_content_w: float32 [2048, 1024], P('user', 'item')
- grad_user_gain: float32 [1024], P('item')
- grad_user_shift: float32 [1024], P('item')
- grad_item_pref_w: float32 [256, 1024], P('item', 'user')
- grad_item_content_w: float32 [2048, 1024], P('item', 'user')
- grad_item_gain: float32 [1024], P('user')
- grad_item_shift: float32 [1024], P('user')
Inputs may be any that keep to these rules, and one draw needn't show every extreme that they name: Batch user r reads table row user_ids[r] + (r // 512) * 1024. Batch item r reads table row item_ids[r] + (r // 256) * 1024.
All inputs are finite; a program needn't handle non-finite values. No bound on the sum of `user_drop` or of `item_drop` on one device may be relied on, other than what follows from the above.
Results may differ from a plain program's by a relative error of at most 0.004.
Values may be sent and summed in bfloat16 or wider, within the bound.
A program may use at most 64 MiB of HBM per device.

v0:
```python
import math

import jax
import jax.numpy as jnp
from jax import lax
from jax.sharding import PartitionSpec as P

EPSILON = 1e-05


def take_rows(table, row_ids, drop_flags):
    chosen = jnp.take(table, row_ids, axis=0)
    keep_rows = (1 - drop_flags).astype(jnp.bfloat16)
    return (chosen, chosen * keep_rows[:, None])


def contract_rows(left, right):
    return lax.dot_general(
        left, right, (((0,), (0,)), ((), ())), preferred_element_type=jnp.float32
    )


def contract_cols(left, right):
    return lax.dot_general(
        left, right, (((1,), (1,)), ((), ())), preferred_element_type=jnp.float32
    )


def activate(centered, col_var, gain, shift):
    inv_std = lax.rsqrt(col_var + EPSILON)
    normed = centered * inv_std
    active = jnp.tanh(normed * gain + shift)
    return (normed, inv_std, active)


def pre_grad(grad_z, normed, inv_std, gain, shift_grad, gain_grad, row_total):
    result = inv_std * (
        grad_z * gain - gain * shift_grad / row_total - normed * (gain * gain_grad / row_total)
    )
    return result.astype(jnp.bfloat16)


def on_device(
    user_table,
    item_table,
    user_ids,
    item_ids,
    user_drop,
    item_drop,
    user_content,
    item_content,
    user_pref_w,
    user_content_w,
    user_gain,
    user_shift,
    item_pref_w,
    item_content_w,
    item_gain,
    item_shift,
):
    users_total = user_ids.shape[0] * lax.axis_size("user")
    items_total = item_ids.shape[0] * lax.axis_size("item")
    user_pref, user_input = take_rows(user_table, user_ids, user_drop)
    item_pref, item_input = take_rows(item_table, item_ids, item_drop)
    user_base = jnp.dot(user_input, user_pref_w, preferred_element_type=jnp.float32)
    item_base = jnp.dot(item_input, item_pref_w, preferred_element_type=jnp.float32)
    user_whole = lax.all_gather(user_content, "item", axis=1, tiled=True)
    item_whole = lax.all_gather(item_content, "user", axis=1, tiled=True)
    user_pre = user_base + jnp.dot(user_whole, user_content_w, preferred_element_type=jnp.float32)
    item_pre = item_base + jnp.dot(item_whole, item_content_w, preferred_element_type=jnp.float32)
    user_total = lax.psum(jnp.sum(user_pre, 0), "user")
    item_total = lax.psum(jnp.sum(item_pre, 0), "item")
    user_center = user_pre - user_total / users_total
    item_center = item_pre - item_total / items_total
    user_spread = lax.psum(jnp.sum(user_center * user_center, 0), "user")
    item_spread = lax.psum(jnp.sum(item_center * item_center, 0), "item")
    user_var = user_spread / users_total
    item_var = item_spread / items_total
    user_normed, user_inv, user_active = activate(user_center, user_var, user_gain, user_shift)
    item_normed, item_inv, item_active = activate(item_center, item_var, item_gain, item_shift)
    user_emb = lax.all_gather(user_active.astype(jnp.bfloat16), "item", axis=1, tiled=True)
    item_emb = lax.all_gather(item_active.astype(jnp.bfloat16), "user", axis=1, tiled=True)
    factor = 1.0 / math.sqrt(user_emb.shape[1])
    loss_weight = 64.0 / math.sqrt(users_total * items_total)
    target = contract_cols(user_pref, item_pref)
    predicted = contract_cols(user_emb, item_emb) * factor
    signal = (loss_weight * (predicted - target)).astype(jnp.bfloat16)
    user_terms = jnp.dot(signal, item_emb, preferred_element_type=jnp.float32) * factor
    item_terms = contract_rows(signal, user_emb) * factor
    user_demb = lax.psum_scatter(user_terms, "item", scatter_dimension=1, tiled=True)
    item_demb = lax.psum_scatter(item_terms, "user", scatter_dimension=1, tiled=True)
    user_dz = user_demb * (1.0 - user_active * user_active)
    item_dz = item_demb * (1.0 - item_active * item_active)
    user_shift_grad, user_gain_grad = lax.psum(
        (jnp.sum(user_dz, 0), jnp.sum(user_dz * user_normed, 0)), "user"
    )
    item_shift_grad, item_gain_grad = lax.psum(
        (jnp.sum(item_dz, 0), jnp.sum(item_dz * item_normed, 0)), "item"
    )
    user_dpre = pre_grad(
        user_dz, user_normed, user_inv, user_gain, user_shift_grad, user_gain_grad, users_total
    )
    item_dpre = pre_grad(
        item_dz, item_normed, item_inv, item_gain, item_shift_grad, item_gain_grad, items_total
    )
    user_pref_term = contract_rows(user_input, user_dpre)
    item_pref_term = contract_rows(item_input, item_dpre)
    user_content_term = contract_rows(user_whole, user_dpre)
    item_content_term = contract_rows(item_whole, item_dpre)
    user_pref_grad, user_content_grad = (
        lax.psum_scatter(user_pref_term, "user", scatter_dimension=0, tiled=True),
        lax.psum_scatter(user_content_term, "user", scatter_dimension=0, tiled=True),
    )
    item_pref_grad, item_content_grad = (
        lax.psum_scatter(item_pref_term, "item", scatter_dimension=0, tiled=True),
        lax.psum_scatter(item_content_term, "item", scatter_dimension=0, tiled=True),
    )
    return (
        user_pref_grad,
        user_content_grad,
        user_gain_grad,
        user_shift_grad,
        item_pref_grad,
        item_content_grad,
        item_gain_grad,
        item_shift_grad,
    )


def solution(mesh):
    in_specs = (
        P("user", None),
        P("item", None),
        P("user"),
        P("item"),
        P("user"),
        P("item"),
        P("user", "item"),
        P("item", "user"),
        P(None, "item"),
        P(None, "item"),
        P("item"),
        P("item"),
        P(None, "user"),
        P(None, "user"),
        P("user"),
        P("user"),
    )
    out_specs = (
        P("user", "item"),
        P("user", "item"),
        P("item"),
        P("item"),
        P("item", "user"),
        P("item", "user"),
        P("user"),
        P("user"),
    )
    return jax.shard_map(
        on_device, mesh=mesh, in_specs=in_specs, out_specs=out_specs, check_vma=False
    )
```

profile of v0, /device:TPU:1, one launch (start us, length us, event | category | flops | bytes accessed | tf_op | source)
XLA Modules:
  0.0 1374.7 jit_solution(7207543735635028089)
XLA Ops:
  7.2 0.0 copy-start
  7.2 0.0 copy-start.6
  7.2 0.0 all-gather.4.cloned.1.call-start
  7.3 0.7 all-gather.4.cloned.1.call-update
  8.0 0.0 all-gather.8.cloned.1.call-start
  8.0 0.7 all-gather.8.cloned.1.call-update
  8.7 0.0 all-gather.6.cloned.1.call-start
  8.8 0.7 compare_select_fusion.1
  9.4 0.7 compare_select_fusion
  10.1 2.1 gather_fusion.1
  12.3 2.0 gather_fusion
  14.2 0.0 copy-start.7
  14.3 0.0 copy-start.9
  14.3 0.0 copy-start.18
  14.4 0.3 fusion.5
  14.7 44.1 %all-gather.4.cloned.1.call-done = bf16[512,2048]{1,0:T(8,128)(2,1)} async-done(((bf16[512,128]{1,0:T(8,128)(2,1)}), bf16[512,2048]{1,0:T(8,128)(2,1)}) %all-gather.4.cloned.1.call-update) | async-done | bytes 2097168 | tf_op jit(solution)/shard_map/all_gather | solution.py:67
  58.8 2.5 fusion.20
  61.3 0.0 copy-start.5
  61.3 70.0 %psum.56 = f32[64]{0:T(128)S(1)} all-reduce(f32[64]{0:T(128)S(1)} %get-tuple-element.38), channel_id=1, replica_groups=mesh['user'=32,'item'=16] {'user'}, use_global_device_ids=true, to_apply=%region_1.2 | all-reduce | flops 64 | bytes 512 | tf_op jit(solution)/shard_map/psum | solution.py:71
  131.3 0.2 multiply_reduce_fusion.1
  131.5 63.2 %psum.57 = f32[64]{0:T(128)S(1)} all-reduce(f32[64]{0:T(128)S(1)} %multiply_reduce_fusion.1), channel_id=1, replica_groups=mesh['user'=32,'item'=16] {'user'}, use_global_device_ids=true, to_apply=%region_3.4 | all-reduce | flops 64 | bytes 512 | tf_op jit(solution)/shard_map/psum | solution.py:75
  194.7 0.7 fusion.13
  195.5 0.0 all-gather.6.cloned.1.call-update
  195.5 0.0 reduce-scatter.10.cloned.1.call-start
  195.6 0.3 fusion.11
  195.9 0.3 fusion.17
  196.2 0.0 all-gather.8.cloned.1.call-done
  196.2 1.6 fusion.21
  197.9 54.3 %psum.58 = f32[32]{0:T(128)S(1)} all-reduce(f32[32]{0:T(128)S(1)} %get-tuple-element.40), channel_id=1, replica_groups=mesh['user'=32,'item'=16] {'item'}, use_global_device_ids=true, to_apply=%region_5.6 | all-reduce | flops 32 | bytes 256 | tf_op jit(solution)/shard_map/psum | solution.py:72
  252.1 0.2 multiply_reduce_fusion.3
  252.3 27.1 %psum.59 = f32[32]{0:T(128)S(1)} all-reduce(f32[32]{0:T(128)S(1)} %multiply_reduce_fusion.3), channel_id=1, replica_groups=mesh['user'=32,'item'=16] {'item'}, use_global_device_ids=true, to_apply=%region_7.8 | all-reduce | flops 32 | bytes 256 | tf_op jit(solution)/shard_map/psum | solution.py:76
  279.5 0.1 fusion.16
  279.6 66.7 %all_gather.15 = bf16[256,1024]{0,1:T(8,128)(2,1)S(1)} all-gather(bf16[256,32]{0,1:T(8,128)(2,1)S(1)} %fusion.16), channel_id=1, replica_groups=mesh['user'=32,'item'=16] {'user'}, dimensions={1}, use_global_device_ids=true | all-gather | bytes 540672 | tf_op jit(solution)/shard_map/all_gather | solution.py:82
  346.3 1.8 fusion.2
  348.1 1.5 convolution_multiply_fusion.1
  349.6 0.0 reduce-scatter.10.cloned.1.call-update
  349.6 0.0 reduce-scatter.8.cloned.1.call-start
  349.6 1.8 convolution_multiply_fusion
  351.4 0.0 reduce-scatter.8.cloned.1.call-update
  351.4 0.0 all-reduce.5.cloned.1.call-start
  351.5 223.1 %reduce-scatter.10.cloned.1.call-done = f32[256,32]{0,1:T(8,128)} async-done(((f32[256,1024]{0,1:T(8,128)}), f32[256,32]{0,1:T(8,128)}) %reduce-scatter.10.cloned.1.call-update) | async-done | bytes 32784 | tf_op jit(solution)/shard_map/reduce_scatter | solution.py:91
  574.6 1.0 fusion.19
  575.6 31.6 %all-reduce.2 = (f32[32]{0:T(128)S(1)}, f32[32]{0:T(128)S(1)}) all-reduce(f32[32]{0:T(128)S(1)} %get-tuple-element.27, f32[32]{0:T(128)S(1)} %get-tuple-element.26), channel_id=1, replica_groups=mesh['user'=32,'item'=16] {'item'}, use_global_device_ids=true, to_apply=%region_19.20 | all-reduce | flops 64 | bytes 512 | tf_op jit(solution)/shard_map/psum | solution.py:97
  607.2 37.2 %reduce-scatter.8.cloned.1.call-done = f32[512,64]{0,1:T(8,128)} async-done(((f32[512,1024]{0,1:T(8,128)}), f32[512,64]{0,1:T(8,128)}) %reduce-scatter.8.cloned.1.call-update) | async-done | bytes 131088 | tf_op jit(solution)/shard_map/reduce_scatter | solution.py:90
  644.4 1.1 fusion.18
  645.5 69.0 %all-reduce.1 = (f32[64]{0:T(128)S(1)}, f32[64]{0:T(128)S(1)}) all-reduce(f32[64]{0:T(128)S(1)} %get-tuple-element.25, f32[64]{0:T(128)S(1)} %get-tuple-element.24), channel_id=1, replica_groups=mesh['user'=32,'item'=16] {'user'}, use_global_device_ids=true, to_apply=%region_12.13 | all-reduce | flops 128 | bytes 1024 | tf_op jit(solution)/shard_map/psum | solution.py:94
  714.6 1.1 fusion.3
  715.7 0.0 all-reduce.5.cloned.1.call-update
  715.7 0.0 reduce-scatter.12.cloned.1.call-start
  715.8 1.0 fusion.9
  716.7 0.0 reduce-scatter.12.cloned.1.call-update
  716.8 0.0 reduce-scatter.14.cloned.1.call-start
  716.8 2.4 convolution_bitcast_fusion.1
  719.2 0.0 reduce-scatter.14.cloned.1.call-update
  719.2 0.0 reduce-scatter.16.cloned.1.call-start
  719.3 0.5 convolution_bitcast_fusion
  719.8 1.3 copy.26
  721.2 0.0 reduce-scatter.16.cloned.1.call-update
  721.2 1.3 dynamic-slice
  723.1 274.4 %all-reduce.5.cloned.1.call-done = f32[256,64]{1,0:T(8,128)} async-done(((f32[256,64]{1,0:T(8,128)}), f32[256,64]{1,0:T(8,128)}) %all-reduce.5.cloned.1.call-update) | async-done | bytes 65552
  997.5 1.3 constant_dynamic-slice_fusion
  998.8 75.9 %reduce-scatter.12.cloned.1.call-done = f32[16,32]{1,0:T(8,128)} async-done(((f32[256,32]{1,0:T(8,128)}), f32[16,32]{1,0:T(8,128)}) %reduce-scatter.12.cloned.1.call-update) | async-done | bytes 2064 | tf_op jit(solution)/shard_map/reduce_scatter | solution.py:115
  1074.8 66.7 %reduce-scatter.14.cloned.1.call-done = f32[128,32]{0,1:T(8,128)} async-done(((f32[2048,32]{0,1:T(8,128)}), f32[128,32]{0,1:T(8,128)}) %reduce-scatter.14.cloned.1.call-update) | async-done | bytes 16400 | tf_op jit(solution)/shard_map/reduce_scatter | solution.py:116
  1141.5 226.7 %reduce-scatter.16.cloned.1.call-done = f32[64,64]{1,0:T(8,128)} async-done(((f32[2048,64]{1,0:T(8,128)}), f32[64,64]{1,0:T(8,128)}) %reduce-scatter.16.cloned.1.call-update) | async-done | bytes 16400
  (45 shorter events, 0.2 us)
Async XLA Ops:
  7.2 5.1 copy-start
  7.2 7.1 copy-start.11
  7.2 7.1 copy-start.6
  7.2 7.1 copy-start.10
  7.2 7.1 copy-start.16
  7.2 51.6 %all-gather.4.cloned.1.call-start = ((), (), s32[]{:S(2)}) async-start(), calls=%async_computation.5 | async-start | bytes 2228224 | tf_op jit(solution)/shard_map/all_gather | solution.py:67
  8.0 188.3 %all-gather.8.cloned.1.call-start = ((), (), s32[]{:S(2)}) async-start(), calls=%async_computation.7 | async-start | bytes 1081344 | tf_op jit(solution)/shard_map/all_gather | solution.py:68
  8.7 337.6 %all-gather.6.cloned.1.call-start = ((), (), s32[]{:S(2)}) async-start(), calls=%async_computation.6 | async-start | bytes 1114112 | tf_op jit(solution)/shard_map/all_gather | solution.py:81
  10.1 48.7 %copy-start.3 = (bf16[2048,64]{0,1:T(8,128)(2,1)S(1)}, bf16[2048,64]{0,1:T(8,128)(2,1)}, u32[]{:S(2)}) copy-start(bf16[2048,64]{0,1:T(8,128)(2,1)} %param.25) | copy-start | bytes 786436
  14.2 180.5 %copy-start.7 = (f32[64]{0:T(128)S(1)}, f32[64]{0:T(128)}, u32[]{:S(2)}) copy-start(f32[64]{0:T(128)} %param.26) | copy-start | bytes 772
  14.3 180.5 %copy-start.9 = (f32[64]{0:T(128)S(1)}, f32[64]{0:T(128)}, u32[]{:S(2)}) copy-start(f32[64]{0:T(128)} %param.27) | copy-start | bytes 772
  14.3 181.3 %copy-start.18 = (s32[256]{0:T(256)S(1)}, s32[256]{0:T(256)}, u32[]{:S(2)}) copy-start(s32[256]{0:T(256)} %param.21) | copy-start | bytes 3076
  14.3 181.3 %copy-start.17 = (bf16[256,32]{0,1:T(8,128)(2,1)S(1)}, bf16[256,32]{0,1:T(8,128)(2,1)}, u32[]{:S(2)}) copy-start(bf16[256,32]{0,1:T(8,128)(2,1)} %param.28) | copy-start | bytes 49156
  14.7 181.5 %copy-start.4 = (bf16[2048,32]{0,1:T(8,128)(2,1)S(1)}, bf16[2048,32]{0,1:T(8,128)(2,1)}, u32[]{:S(2)}) copy-start(bf16[2048,32]{0,1:T(8,128)(2,1)} %param.29) | copy-start | bytes 393220
  61.3 218.2 %copy-start.5 = (f32[32]{0:T(128)S(1)}, f32[32]{0:T(128)}, u32[]{:S(2)}) copy-start(f32[32]{0:T(128)} %param.30) | copy-start | bytes 388
  61.3 218.2 %copy-start.8 = (f32[32]{0:T(128)S(1)}, f32[32]{0:T(128)}, u32[]{:S(2)}) copy-start(f32[32]{0:T(128)} %param.31) | copy-start | bytes 388
  195.5 379.1 %reduce-scatter.10.cloned.1.call-start = ((), (), s32[]{:S(2)}) async-start(), calls=%async_computation.9 | async-start | bytes 1081344 | tf_op jit(solution)/shard_map/reduce_scatter | solution.py:91
  346.3 1.8 copy-start.2
  349.6 294.8 %reduce-scatter.8.cloned.1.call-start = ((), (), s32[]{:S(2)}) async-start(), calls=%async_computation.8 | async-start | bytes 2228224 | tf_op jit(solution)/shard_map/reduce_scatter | solution.py:90
  351.4 367.8 %copy-start.1 = (bf16[512,2048]{1,0:T(8,128)(2,1)S(1)}, bf16[512,2048]{1,0:T(8,128)(2,1)}, u32[]{:S(2)}) copy-start(bf16[512,2048]{1,0:T(8,128)(2,1)} %all-gather.4.cloned.1.call-done) | copy-start | bytes 6291460
  351.4 646.1 %all-reduce.5.cloned.1.call-start = ((), (), s32[]{:S(2)}) async-start(), calls=%async_computation.13 | async-start | bytes 262144
  607.2 112.6 %copy-start.12 = (f32[32]{0:T(128)}, f32[32]{0:T(128)S(1)}, u32[]{:S(2)}) copy-start(f32[32]{0:T(128)S(1)} %get-tuple-element.30) | copy-start | bytes 388
  607.2 112.6 %copy-start.13 = (f32[32]{0:T(128)}, f32[32]{0:T(128)S(1)}, u32[]{:S(2)}) copy-start(f32[32]{0:T(128)S(1)} %get-tuple-element.31) | copy-start | bytes 388
  714.5 5.3 copy-start.14
  714.5 5.3 copy-start.15
  715.7 359.1 %reduce-scatter.12.cloned.1.call-start = ((), (), s32[]{:S(2)}) async-start(), calls=%async_computation.10 | async-start | bytes 139264 | tf_op jit(solution)/shard_map/reduce_scatter | solution.py:115
  716.8 424.7 %reduce-scatter.14.cloned.1.call-start = ((), (), s32[]{:S(2)}) async-start(), calls=%async_computation.11 | async-start | bytes 278528 | tf_op jit(solution)/shard_map/reduce_scatter | solution.py:116
  719.2 649.0 %reduce-scatter.16.cloned.1.call-start = ((), (), s32[]{:S(2)}) async-start(), calls=%async_computation.12 | async-start | bytes 1081344
Sparse Core Ops, SparseCore 0:
  10.1 48.6 all-gather.3
  62.0 77.8 all-gather.7
  195.6 59.5 all-gather.5
  349.7 224.8 reduce-scatter.9
  577.3 67.0 reduce-scatter.7
  715.8 281.6 all-reduce.4
  1001.1 73.5 reduce-scatter.11
  1078.1 63.3 reduce-scatter.13
  1147.1 221.0 reduce-scatter.15
where the time goes:
time: 1380 us; the launch traced here: 1370 us
  waiting for transfers between devices  950 us (69%)
  blocking collectives  382 us (28%)
  matrix products  15 us (1%)
  between operations  14.8 us (1%)
    unnamed x11, waiting for transfers between devices  503 us
    reduce_scatter x1, waiting for transfers between devices, on_device(): lax.psum_scatter(item_terms, 'user', scatter_dimension=1, tiled=True)  223 us
    reduce_scatter x1, waiting for transfers between devices, on_device(): lax.psum_scatter(item_pref_term, 'item', scatter_dimension=0, tiled=True)  75.9 us
    psum x1, blocking collectives, on_device(): user_total = lax.psum(jnp.sum(user_pre, 0), 'user')  70 us
    psum x1, blocking collectives, on_device(): lax.psum((jnp.sum(user_dz, 0), jnp.sum(user_dz * user_normed, 0)), 'user')  69 us
    reduce_scatter x1, waiting for transfers between devices, on_device(): lax.psum_scatter(item_content_term, 'item', scatter_dimension=0, tiled=True)  66.7 us
    all_gather x1, blocking collectives, on_device(): lax.all_gather(item_active.astype(jnp.bfloat16), 'user', axis=1, tiled=True)  66.7 us
    psum x1, blocking collectives, on_device(): user_spread = lax.psum(jnp.sum(user_center * user_center, 0), 'user')  63.2 us
  transfers between devices with their start and end apart: 9, of which 7 were waited for; matrix products, arithmetic and copies ran while one was open for 2% of the time, Pallas kernels for 0%

commit v1 on v0

v1 whole, which is shorter than its diff:
```python
import functools
import math

import jax
import jax.numpy as jnp
from jax import lax
from jax.experimental import pallas as pl
from jax.experimental.pallas import tpu as pltpu
from jax.sharding import PartitionSpec as P

EPSILON = 1e-05
YH, Z, YL, X, C = 4, 8, 2, 4, 2
N_USER, N_ITEM, CHIPS = YH * Z, YL * X * C, YL * X
USERS, ITEMS, HID, RANK, CONTENT = 16384, 4096, 1024, 256, 2048
UB = 256
IB = 256
UH = 128
IH = 32
BF, F32 = jnp.bfloat16, jnp.float32
MESH = pl.DeviceIdType.MESH

NN = (((1,), (0,)), ((), ()))
NT = (((1,), (1,)), ((), ()))
TN = (((0,), (0,)), ((), ()))


def dot(left, right, dims=NN):
    return lax.dot_general(left, right, dims, preferred_element_type=F32)


class Counter:
    def __init__(self):
        self.count = 0

    def take(self, amount=1):
        self.count += amount
        return self.count - amount


def kernel(
    ut, it, uid, iid, udrop, idrop, uc, ic, upw, ucw, ugain, ushift, ipw, icw, igain, ishift,
    o_upw, o_ucw, o_ug, o_us, o_ipw, o_icw, o_ig, o_is,
    xb, cT, wdup, wsib, wU, gsd, gss, wT3, ipref, upref, uinp, iinp, su, sz, si, ue, eb, tgt, sig, tbs, sb, tf,
    utf, utb, r1, r2, ys, yr, isd, ir, zs, zr, du, dz8, di, pk, ps, pc, pz, pys, pyr, gi, gr,
    ssem, rsem,
):
    u, i = lax.axis_index("user"), lax.axis_index("item")
    yh, z = lax.div(u, Z), lax.rem(u, Z)
    yl, x, c = lax.div(i, X * C), lax.rem(lax.div(i, C), X), lax.rem(i, C)
    sent, landed, pending = Counter(), Counter(), []

    def at(dyh=0, dz=0, dyl=0, dx=0, dc=0):
        return {
            "user": lax.rem(yh + dyh, YH) * Z + lax.rem(z + dz + Z, Z),
            "item": lax.rem(yl + dyl, YL) * (X * C) + lax.rem(x + dx + X, X) * C + lax.rem(c + dc, C),
        }

    def YHI(d):
        return lax.rem(yh + d + YH, YH)

    def ZI(d):
        return lax.rem(z + d + Z, Z)

    def XI(d):
        return lax.rem(x + d + X, X)

    def CHIP(row, d):
        return lax.rem(yl + row, YL) * X + XI(d)

    def CI(r):
        return lax.rem(c + r, C)

    def send(src, dst, device, landing):
        copy = pltpu.make_async_remote_copy(
            src_ref=src, dst_ref=dst, send_sem=ssem.at[sent.take()], recv_sem=rsem.at[landing],
            device_id=device, device_id_type=MESH,
        )
        copy.start()
        pending.append(copy)

    def recv(dst, landing):
        pltpu.make_async_remote_copy(
            src_ref=dst, dst_ref=dst, send_sem=ssem.at[0], recv_sem=rsem.at[landing],
            device_id=at(dc=1), device_id_type=MESH,
        ).wait_recv()

    barrier = pltpu.get_barrier_semaphore()
    peers = [dict(dyl=a, dx=b, dc=r) for a in range(YL) for b in range(X) for r in range(C) if a or b or r]
    peers += [dict(dz=d) for d in range(1, Z)]
    peers += [dict(dyh=e, dc=r) for e in range(1, YH) for r in range(C)]
    for peer in peers:
        pl.semaphore_signal(barrier, inc=1, device_id=at(**peer), device_id_type=MESH)

    def eye(n):
        return (
            lax.broadcasted_iota(jnp.int32, (n, n), 0) == lax.broadcasted_iota(jnp.int32, (n, n), 1)
        ).astype(F32).astype(BF)

    cT[yh, z] = dot(eye(64), ic[...], NT).astype(BF)
    xb[CHIP(0, 0), c] = uc[pl.ds(pl.multiple_of(c * UB, UB), UB), :]
    lane = lax.broadcasted_iota(jnp.int32, (1, 128), 1)
    low = lane < 64
    mine_mask = low == (c == 0)

    def twice(v):
        return jnp.concatenate([v, v], axis=1)

    wdup[0:CONTENT, :] = twice(ucw[...])
    wdup[CONTENT:, :] = twice(upw[...])
    sub8 = lax.broadcasted_iota(jnp.int32, (8, 128), 0)
    gsd[...] = jnp.where(sub8 == 0, twice(ugain[...]), twice(ushift[...]))

    pl.semaphore_wait(barrier, len(peers))

    n_iy = landed.take(YH)
    n_iz = [[landed.take(YH) for _ in range(Z // 2)] for _ in range(2)]
    n_w, n_gs, n_pref, n_us = landed.take(), landed.take(), landed.take(), landed.take()
    n_uy = landed.take(2)
    n_ux = [[[landed.take(2) for _ in range(2)] for _ in range(2)] for _ in range(2)]

    def item_y(buf):
        for e in range(1, YH):
            send(buf.at[yh, z], buf.at[yh, z], at(dyh=e), n_iy + e)

    def item_z(buf, base, step, e, direction):
        if step < Z // 2 or (e < 2) == (direction == 1):
            k = 0 if direction == 1 else 1
            slot = buf.at[YHI(-e), ZI(-direction * (step - 1))]
            send(slot, slot, at(dz=direction), base[k][step - 1] + e)

    def item_z_wait(buf, base, step, e, direction):
        if step < Z // 2 or (e < 2) == (direction == 1):
            k = 0 if direction == 1 else 1
            recv(buf.at[YHI(-e), ZI(-direction * step)], base[k][step - 1] + e)

    def user_slot(buf, row, d, piece, relative):
        return buf.at[CHIP(row, d), CI(piece) if relative else piece]

    def user_x_forward(buf, base, row, relative):
        for direction, piece in ((1, 0), (-1, 1)):
            k = 0 if direction == 1 else 1
            slot = user_slot(buf, row, -direction, piece, relative)
            recv(slot, base[row][k][0] + piece)
            send(slot, slot, at(dx=direction), base[row][k][1] + piece)

    def user_x_rest(buf, base, row, relative):
        for direction, piece in ((1, 1), (-1, 0)):
            k = 0 if direction == 1 else 1
            recv(user_slot(buf, row, -direction, piece, relative), base[row][k][0] + piece)

    def user_x_far(buf, base, row, relative):
        recv(user_slot(buf, row, 2, 0, relative), base[row][0][1] + 0)
        recv(user_slot(buf, row, 2, 1, relative), base[row][1][1] + 1)

    item_z(cT, n_iz, 1, 0, 1)
    item_z(cT, n_iz, 1, 0, -1)
    for r in range(C):
        half = uc.at[pl.ds(pl.multiple_of(CI(r) * UB, UB), UB), :]
        slot = xb.at[CHIP(0, 0), c]
        for direction in (1, -1):
            send(half, slot, at(dx=direction, dc=r), n_ux[0][0 if direction == 1 else 1][0] + r)
        send(half, slot, at(dyl=1, dc=r), n_uy + r)
        if r:
            send(half, slot, at(dc=1), n_us)
    item_y(cT)
    send(wdup, wsib, at(dc=1), n_w)
    send(gsd, gss, at(dc=1), n_gs)

    for zz in range(Z):
        rows = jnp.concatenate([icw[(a * Z + zz) * 64:(a * Z + zz + 1) * 64, :] for a in range(YH)], axis=0)
        wT3[zz] = dot(eye(IH), rows, NT).astype(BF)
    for e in range(1, YH):
        recv(cT.at[YHI(-e), z], n_iy + e)
        item_z(cT, n_iz, 1, e, 1)
        item_z(cT, n_iz, 1, e, -1)
    for r in range(C):
        slot = user_slot(xb, 1, 0, r, True)
        recv(slot, n_uy + r)
        for direction in (1, -1):
            send(slot, slot, at(dx=direction), n_ux[1][0 if direction == 1 else 1][0] + r)
    user_x_forward(xb, n_ux, 0, True)

    def column(row):
        return jnp.broadcast_to(row.astype(F32), (128, 256)).T

    def take(table, ids, drop):
        ids, keep = column(ids), 1.0 - column(drop)
        places = lax.broadcasted_iota(jnp.int32, (256, 128), 1).astype(F32)
        one_hot = jnp.concatenate(
            [(ids == places + 128.0 * t).astype(F32).astype(BF) for t in range(8)], axis=1
        )
        chosen = dot(one_hot, table)
        return chosen.astype(BF), (chosen * jnp.concatenate([keep, keep], axis=1)).astype(BF)

    chosen, kept = take(it[...], iid[...], idrop[...])
    ipref[c] = chosen
    iinp[...] = kept
    send(ipref.at[c], ipref.at[c], at(dc=1), n_pref)

    for e in range(YH):
        for direction in (1, -1):
            item_z_wait(cT, n_iz, 1, e, direction)
            item_z(cT, n_iz, 2, e, direction)
    user_x_forward(xb, n_ux, 1, True)

    mine = c == 0
    chosen, kept = take(
        ut[...],
        jnp.where(mine, uid[:, 0:UB], uid[:, UB:]),
        jnp.where(mine, udrop[:, 0:UB], udrop[:, UB:]),
    )
    upref[...] = chosen
    uinp[...] = kept
    recv(wsib, n_w)
    recv(gss, n_gs)
    wU[...] = jnp.where(mine_mask, wdup[...].astype(F32), wsib[...].astype(F32)).astype(BF)
    gain_shift = jnp.where(mine_mask, gsd[...], gss[...])
    gain, shift = gain_shift[0:1, :], gain_shift[1:2, :]
    ipwT = dot(eye(IH), ipw[...], NT).astype(BF)
    preT = dot(ipwT, iinp[...], NT)
    pre = dot(uinp[...], wU[CONTENT:, :])

    def item_part(zi):
        return dot(wT3[zi], jnp.concatenate([cT[a, zi] for a in range(YH)], axis=0))

    def user_part(chip):
        rows = wU[pl.ds(pl.multiple_of(chip * 256, 256), 256), :]
        return dot(jnp.concatenate([xb[chip, 0], xb[chip, 1]], axis=1), rows)

    for e in range(YH):
        for direction in (1, -1):
            item_z_wait(cT, n_iz, 2, e, direction)
            item_z(cT, n_iz, 3, e, direction)
    preT += item_part(z)
    preT += item_part(ZI(1))
    preT += item_part(ZI(-1))
    recv(user_slot(xb, 0, 0, 1, True), n_us)
    pre += user_part(CHIP(0, 0))
    pre += user_part(CHIP(1, 0))
    user_x_rest(xb, n_ux, 0, True)
    pre += user_part(CHIP(0, 1))
    pre += user_part(CHIP(0, -1))
    user_x_far(xb, n_ux, 0, True)
    pre += user_part(CHIP(0, 2))
    for e in range(YH):
        for direction in (1, -1):
            item_z_wait(cT, n_iz, 3, e, direction)
            item_z(cT, n_iz, 4, e, direction)
    preT += item_part(ZI(2))
    preT += item_part(ZI(-2))
    user_x_rest(xb, n_ux, 1, True)
    pre += user_part(CHIP(1, 1))
    pre += user_part(CHIP(1, -1))
    user_x_far(xb, n_ux, 1, True)
    pre += user_part(CHIP(1, 2))

    n_su, n_sz, n_si = landed.take(YH * C), landed.take(Z), landed.take(N_ITEM)

    def rows_of(*rows):
        result = jnp.zeros((8, 128), F32)
        for k, row in enumerate(rows):
            result = jnp.where(sub8 == k, row, result)
        return result

    def user_first(buf, base):
        for e in range(YH):
            for r in range(C):
                if e or r:
                    send(buf.at[yh, c], buf.at[yh, c], at(dyh=e, dc=r), base + e * C + r)

    def user_first_wait(buf, base):
        for e in range(YH):
            for r in range(C):
                if e or r:
                    recv(buf.at[YHI(-e), CI(r)], base + e * C + r)

    def user_second(buf, base):
        for d in range(1, Z):
            send(buf.at[z], buf.at[z], at(dz=d), base + d)

    def user_second_wait(buf, base):
        for d in range(1, Z):
            recv(buf.at[ZI(-d)], base + d)

    def item_all(buf, base):
        for a in range(YL):
            for b in range(X):
                for r in range(C):
                    if a or b or r:
                        send(buf.at[i], buf.at[i], at(dyl=a, dx=b, dc=r), base + (a * X + b) * C + r)

    def item_all_wait(buf, base):
        for a in range(YL):
            for b in range(X):
                for r in range(C):
                    if a or b or r:
                        recv(buf.at[CHIP(a, -b) * C + CI(r)], base + (a * X + b) * C + r)

    def to_rows(first, second):
        both = jnp.where(lane == 0, first, jnp.where(lane == 1, second, 0.0))
        return jnp.concatenate([both, jnp.zeros((96, 128), F32)], axis=0).T[0:8, :]

    def to_columns(rows):
        full = jnp.concatenate([rows, jnp.zeros((120, 128), F32)], axis=0).T
        return full[0:IH, 0:1], full[0:IH, 1:2]

    mean = jnp.sum(pre, 0, keepdims=True) * (1.0 / UB)
    gap = pre - mean
    su[yh, c] = rows_of(mean, jnp.sum(gap * gap, 0, keepdims=True))
    user_first(su, n_su)

    for e in range(YH):
        for direction in (1, -1):
            item_z_wait(cT, n_iz, 4, e, direction)
    preT += item_part(ZI(3))
    preT += item_part(ZI(-3))
    preT += item_part(ZI(4))
    imean = jnp.sum(preT, 1, keepdims=True) * (1.0 / IB)
    gap = preT - imean
    si[i] = to_rows(imean, jnp.sum(gap * gap, 1, keepdims=True))
    item_all(si, n_si)

    def combine(means, squares, each):
        total = sum(means[1:], means[0]) * (1.0 / len(means))
        spread = sum(squares[1:], squares[0])
        apart = [(m - total) * (m - total) for m in means]
        return total, spread + float(each) * sum(apart[1:], apart[0])

    user_first_wait(su, n_su)
    blocks = [su[a, r] for a in range(YH) for r in range(C)]
    mean, spread = combine([b[0:1] for b in blocks], [b[1:2] for b in blocks], UB)
    sz[z] = rows_of(mean, spread)
    user_second(sz, n_sz)
    recv(ipref.at[CI(1)], n_pref)
    for r in range(C):
        tgt[r] = dot(upref[...], ipref[r], NT)
    item_all_wait(si, n_si)
    blocks = [si[k] for k in range(N_ITEM)]
    imean, ispread = combine([b[0:1] for b in blocks], [b[1:2] for b in blocks], IB)
    imean, iinv = to_columns(rows_of(imean, lax.rsqrt(ispread * (1.0 / ITEMS) + EPSILON)))

    n_ey = landed.take(YH)
    n_ez = [[landed.take(YH) for _ in range(Z // 2)] for _ in range(2)]
    n_es = landed.take(Z)
    n_vy = landed.take(2)
    n_vx = [[[landed.take(2) for _ in range(2)] for _ in range(2)] for _ in range(2)]

    def as_column(row):
        square = jnp.broadcast_to(row, (IH, IH))
        diagonal = lax.broadcasted_iota(jnp.int32, (IH, IH), 0) == lax.broadcasted_iota(jnp.int32, (IH, IH), 1)
        return jnp.sum(jnp.where(diagonal, square, 0.0), 1, keepdims=True)

    igain_c, ishift_c = as_column(igain[...]), as_column(ishift[...])
    inorm = (preT - imean) * iinv
    iact = jnp.tanh(inorm * igain_c + ishift_c)
    ebc = eb.at[c]
    ebc[yh, z] = iact.astype(BF)
    item_z(ebc, n_ez, 1, 0, 1)
    item_z(ebc, n_ez, 1, 0, -1)
    for e in range(1, YH):
        send(ebc.at[yh, z], ebc.at[yh, z], at(dyh=e), n_ey + e)

    user_second_wait(sz, n_sz)
    blocks = [sz[k] for k in range(Z)]
    mean, spread = combine([b[0:1] for b in blocks], [b[1:2] for b in blocks], UB * YH * C)
    inv = lax.rsqrt(spread * (1.0 / USERS) + EPSILON)
    norm = (pre - mean) * inv
    act = jnp.tanh(norm * gain + shift)
    emb = act.astype(BF)
    own = CHIP(0, 0)
    ue[own, 0] = emb[0:128, :]
    ue[own, 1] = emb[128:256, :]
    for h in range(2):
        for direction in (1, -1):
            send(ue.at[own, h], ue.at[own, h], at(dx=direction), n_vx[0][0 if direction == 1 else 1][0] + h)
        send(ue.at[own, h], ue.at[own, h], at(dyl=1), n_vy + h)

    def share(group, k):
        send(ebc.at[:, group], ebc.at[:, group], at(dc=1), n_es + k)

    for e in range(1, YH):
        recv(ebc.at[YHI(-e), z], n_ey + e)
        item_z(ebc, n_ez, 1, e, 1)
        item_z(ebc, n_ez, 1, e, -1)
    share(z, 0)
    for h in range(2):
        slot = ue.at[CHIP(1, 0), h]
        recv(slot, n_vy + h)
        for direction in (1, -1):
            send(slot, slot, at(dx=direction), n_vx[1][0 if direction == 1 else 1][0] + h)
    user_x_forward(ue, n_vx, 0, False)
    for step in range(1, Z // 2):
        for e in range(YH):
            for direction in (1, -1):
                item_z_wait(ebc, n_ez, step, e, direction)
                item_z(ebc, n_ez, step + 1, e, direction)
        share(ZI(-step), 2 * step - 1)
        share(ZI(step), 2 * step)
        if step == 1:
            user_x_forward(ue, n_vx, 1, False)
    for row in range(YL):
        user_x_rest(ue, n_vx, row, False)
        user_x_far(ue, n_vx, row, False)
    for e in range(YH):
        for direction in (1, -1):
            item_z_wait(ebc, n_ez, Z // 2, e, direction)
    share(ZI(4), 7)
    ebs = eb.at[CI(1)]
    recv(ebs.at[:, z], n_es)
    for step in range(1, Z // 2):
        recv(ebs.at[:, ZI(-step)], n_es + 2 * step - 1)
        recv(ebs.at[:, ZI(step)], n_es + 2 * step)
    recv(ebs.at[:, ZI(4)], n_es + 7)

    n_sb = landed.take(YH)
    n_r1, n_r2, n_yr = landed.take(2), landed.take(4), landed.take()
    n_ir = [[landed.take(2) for _ in range(Z // 2)] for _ in range(2)]
    n_zr = landed.take(YH)
    factor = 1.0 / math.sqrt(HID)
    loss_weight = 64.0 / math.sqrt(USERS * ITEMS)

    def user_rows(k):
        return jnp.concatenate([ue[k, 0], ue[k, 1]], axis=0)

    def item_rows(r, k):
        return eb[r, k].reshape(256, IB)

    for r in range(C):
        score = tgt[r] * (-1.0)
        total = None
        for k in range(4):
            part = dot(jnp.concatenate([user_rows(2 * k), user_rows(2 * k + 1)], axis=1), item_rows(r, k))
            total = part if total is None else total + part
        sig[r] = (loss_weight * (total * factor + score)).astype(BF)

    def item_term(signal, k):
        both = jnp.concatenate([user_rows(2 * k), user_rows(2 * k + 1)], axis=1)
        return dot(both, signal, TN) * factor

    other = sig[CI(1)]
    for k in range(YH):
        tbs[k] = item_term(other, k).astype(BF).reshape(Z, IH, IB)
        send(tbs.at[k], sb.at[k], at(dc=1), n_sb + k)

    def user_term(chip):
        rows = lax.div(chip, 2), lax.rem(chip, 2) * 4
        total = None
        for r in range(C):
            part = dot(sig[r], eb[r, rows[0], pl.ds(rows[1], 4)].reshape(UH, IB), NT)
            total = part if total is None else total + part
        return total * factor

    def put_term(a, d):
        term = user_term(a * X + XI(d)).reshape(2, 128, 128)
        utf[a, XI(d)] = term
        utb[a, XI(d)] = term.astype(BF)

    for a in range(YL):
        put_term(a, 2)
    send(utb.at[:, XI(2), 0], r1.at[0], at(dx=1), n_r1)
    send(utb.at[:, XI(2), 1], r1.at[1], at(dx=-1), n_r1 + 1)
    for a in range(YL):
        put_term(a, 1)
        put_term(a, -1)
    send(utb.at[:, XI(1), 1], r2.at[0, 1], at(dx=1), n_r2 + 1)
    send(utb.at[:, XI(-1), 0], r2.at[1, 0], at(dx=-1), n_r2 + 2)
    own_signal = sig[c]
    for k in range(YH):
        tf[k] = item_term(own_signal, k).reshape(Z, IH, IB)
    for k, d in ((0, 1), (1, -1)):
        recv(r1.at[k], n_r1 + k)
        utb[:, XI(d), k] = (utf[:, XI(d), k] + r1[k].astype(F32)).astype(BF)
        send(utb.at[:, XI(d), k], r2.at[k, k], at(dx=d), n_r2 + 2 * k + k)
    for k in range(YH):
        recv(sb.at[k], n_sb + k)
        tf[k] = tf[k] + sb[k].astype(F32)
    for k, d in ((0, 1), (1, -1)):
        h = k
        isd[k, 0, h] = tf[2 * h:2 * h + 2, ZI(4)].astype(BF)
        send(isd.at[k, 0, h], ir.at[k, 0, h], at(dz=d), n_ir[k][0] + h)
    for k, d in ((0, 1), (1, -1)):
        h = 1 - k
        isd[k, 1, h] = tf[2 * h:2 * h + 2, ZI(3 * d)].astype(BF)
        send(isd.at[k, 1, h], ir.at[k, 1, h], at(dz=d), n_ir[k][1] + h)
    for a in range(YL):
        put_term(a, 0)
    for step in range(2, Z // 2 + 1):
        for hh in range(2):
            for k, d in ((0, 1), (1, -1)):
                h = hh if k == 0 else 1 - hh
                if step == 2 and hh == 1:
                    continue
                recv(ir.at[k, step - 2, h], n_ir[k][step - 2] + h)
                isd[k, step - 1, h] = (
                    tf[2 * h:2 * h + 2, ZI((5 - step) * d)] + ir[k, step - 2, h].astype(F32)
                ).astype(BF)
                send(isd.at[k, step - 1, h], ir.at[k, step - 1, h], at(dz=d), n_ir[k][step - 1] + h)
        if step == 2:
            for k in range(2):
                for h in range(2):
                    recv(r2.at[k, h], n_r2 + 2 * k + h)
            for a in range(YL):
                for h in range(2):
                    utf[a, x, h] = utf[a, x, h] + r2[0, h, a].astype(F32) + r2[1, h, a].astype(F32)
            ys[...] = utf[lax.rem(yl + 1, YL), x].astype(BF)
            send(ys, yr, at(dyl=1), n_yr)
    recv(yr, n_yr)
    demb = (utf[yl, x] + yr[...].astype(F32)).reshape(UB, UH)

    n_du, n_d8, n_di = landed.take(YH * C), landed.take(Z), landed.take(N_ITEM)
    dz = demb * (1.0 - act * act)
    du[yh, c] = rows_of(jnp.sum(dz, 0, keepdims=True), jnp.sum(dz * norm, 0, keepdims=True))
    user_first(du, n_du)
    for h in range(2):
        for k in range(2):
            recv(ir.at[k, 3, h], n_ir[k][3] + h)
        part = tf[2 * h:2 * h + 2, z] + ir[0, 3, h].astype(F32) + ir[1, 3, h].astype(F32)
        tf[2 * h:2 * h + 2, z] = part
        zs[2 * h:2 * h + 2] = part.astype(BF)
    for e in range(1, YH):
        send(zs.at[YHI(e)], zr.at[yh], at(dyh=e), n_zr + e)
    user_first_wait(du, n_du)
    dz8[z] = sum([du[a, r] for a in range(YH) for r in range(C)][1:], du[0, 0])
    user_second(dz8, n_d8)
    dembT = tf[yh, z]
    for e in range(1, YH):
        recv(zr.at[YHI(-e)], n_zr + e)
        dembT += zr[YHI(-e)].astype(F32)
    idz = dembT * (1.0 - iact * iact)
    di[i] = to_rows(jnp.sum(idz, 1, keepdims=True), jnp.sum(idz * inorm, 1, keepdims=True))
    item_all(di, n_di)
    user_second_wait(dz8, n_d8)
    sums = sum([dz8[k] for k in range(1, Z)], dz8[0])
    s_sum, g_sum = sums[0:1, :], sums[1:2, :]
    for out, row in ((o_us, s_sum), (o_ug, g_sum)):
        out[...] = jnp.where(mine, row[:, 0:64], row[:, 64:128])

    n_ps, n_pz, n_py, n_gr = landed.take(), landed.take(Z), landed.take(YH), landed.take(N_ITEM)
    dpre = (
        inv * (dz * gain - gain * s_sum * (1.0 / USERS) - norm * (gain * g_sum * (1.0 / USERS)))
    ).astype(BF)

    def turn(v):
        return pltpu.roll(v, 64, 1)

    pref = dot(uinp[...], dpre, TN)
    pref_turned = turn(pref)
    blank = jnp.zeros((8, 128), F32)
    for k in range(CHIPS):
        block = dot(jnp.concatenate([xb[k, 0], xb[k, 1]], axis=1), dpre, TN)
        for q in range(4):
            uu = 4 * k + q
            first, second = block[64 * q:64 * q + 32], block[64 * q + 32:64 * q + 64]
            pk[0, uu] = jnp.concatenate(
                [jnp.where(low, first, turn(second)), pref[8 * uu:8 * uu + 8], blank], axis=0
            ).astype(BF)
            pk[1, uu] = jnp.concatenate(
                [jnp.where(low, turn(first), second), pref_turned[8 * uu:8 * uu + 8], blank], axis=0
            ).astype(BF)
    send(pk.at[CI(1)], ps, at(dc=1), n_ps)

    item_all_wait(di, n_di)
    sums = sum([di[k] for k in range(1, N_ITEM)], di[0])
    o_is[...] = sums[0:1, 0:IH]
    o_ig[...] = sums[1:2, 0:IH]
    is_sum, ig_sum = to_columns(sums)
    idpre = (
        iinv * (idz * igain_c - igain_c * is_sum * (1.0 / ITEMS) - inorm * (igain_c * ig_sum * (1.0 / ITEMS)))
    ).astype(BF)
    ipg = dot(idpre, iinp[...])
    ipg = jnp.concatenate([ipg, jnp.zeros((96, RANK), F32)], axis=0).T
    for k in range(N_ITEM):
        block = dot(idpre, cT[k // 4, 2 * (k % 4):2 * (k % 4) + 2].reshape(128, IB), NT)
        gi[k] = jnp.concatenate([block, ipg[16 * k:16 * k + 16]], axis=0).astype(BF)
    for a in range(YL):
        for b in range(X):
            for r in range(C):
                if a or b or r:
                    send(
                        gi.at[CHIP(a, b) * C + CI(r)], gr.at[i], at(dyl=a, dx=b, dc=r),
                        n_gr + (a * X + b) * C + r,
                    )
    recv(ps, n_ps)
    pc[...] = (pk[c].astype(F32) + ps[...].astype(F32)).astype(BF).reshape(YH, Z, 48, 128)
    for d in range(1, Z):
        send(pc.at[:, ZI(d)], pz.at[z], at(dz=d), n_pz + d)

    total = gi[i].astype(F32)
    for a in range(YL):
        for b in range(X):
            for r in range(C):
                if a or b or r:
                    slot = CHIP(a, -b) * C + CI(r)
                    recv(gr.at[slot], n_gr + (a * X + b) * C + r)
                    total += gr[slot].astype(F32)
    o_icw[...] = jnp.concatenate([total[0:IH], jnp.zeros((96, 128), F32)], axis=0).T[:, 0:IH]
    o_ipw[...] = total[IH:, 0:IH]

    part = pc[:, z].astype(F32)
    for d in range(1, Z):
        recv(pz.at[ZI(-d)], n_pz + d)
        part += pz[ZI(-d)].astype(F32)
    pys[...] = part.astype(BF)
    for e in range(1, YH):
        send(pys.at[YHI(e)], pyr.at[yh], at(dyh=e), n_py + e)
    total = pys[yh].astype(F32)
    for e in range(1, YH):
        recv(pyr.at[YHI(-e)], n_py + e)
        total += pyr[YHI(-e)].astype(F32)
    o_ucw[0:32, :] = total[0:32, 0:64]
    o_ucw[32:64, :] = total[0:32, 64:128]
    o_upw[...] = total[32:40, 0:64]

    for copy in pending:
        copy.wait_send()
    kernel.counts = sent.count, landed.count


SCRATCH = dict(
    xb=((CHIPS, 2, UB, 128), BF), cT=((YH, Z, 64, IB), BF), wdup=((2304, 128), BF), wsib=((2304, 128), BF),
    wU=((2304, 128), BF), gsd=((8, 128), F32), gss=((8, 128), F32), wT3=((Z, IH, 256), BF),
    ipref=((2, IB, RANK), BF), upref=((UB, RANK), BF), uinp=((UB, RANK), BF), iinp=((IB, RANK), BF),
    su=((YH, C, 8, 128), F32), sz=((Z, 8, 128), F32), si=((N_ITEM, 8, 128), F32),
    ue=((CHIPS, 2, 128, 128), BF), eb=((2, YH, Z, IH, IB), BF), tgt=((2, UB, IB), F32), sig=((2, UB, IB), BF),
    tbs=((YH, Z, IH, IB), BF), sb=((YH, Z, IH, IB), BF), tf=((YH, Z, IH, IB), F32),
    utf=((YL, X, 2, 128, 128), F32), utb=((YL, X, 2, 128, 128), BF), r1=((2, YL, 128, 128), BF),
    r2=((2, 2, YL, 128, 128), BF), ys=((2, 128, 128), BF), yr=((2, 128, 128), BF),
    isd=((2, 4, 2, 2, IH, IB), BF), ir=((2, 4, 2, 2, IH, IB), BF), zs=((YH, IH, IB), BF), zr=((YH, IH, IB), BF),
    du=((YH, C, 8, 128), F32), dz8=((Z, 8, 128), F32), di=((N_ITEM, 8, 128), F32),
    pk=((2, N_USER, 48, 128), BF), ps=((N_USER, 48, 128), BF), pc=((YH, Z, 48, 128), BF),
    pz=((Z, YH, 48, 128), BF), pys=((YH, 48, 128), BF), pyr=((YH, 48, 128), BF),
    gi=((N_ITEM, 48, 128), BF), gr=((N_ITEM, 48, 128), BF),
)


def on_device(ut, it, uid, iid, udrop, idrop, uc, ic, upw, ucw, ugain, ushift, ipw, icw, igain, ishift):
    def row(v):
        return v.reshape(1, v.shape[0])

    args = (ut, it, row(uid), row(iid), row(udrop), row(idrop), uc, ic, upw, ucw, row(ugain), row(ushift),
            ipw, icw, row(igain), row(ishift))
    shapes = [(8, 64), (64, 64), (1, 64), (1, 64), (16, 32), (128, 32), (1, 32), (1, 32)]
    vmem = pl.BlockSpec(memory_space=pltpu.VMEM)
    outs = pl.pallas_call(
        kernel,
        out_shape=[jax.ShapeDtypeStruct(s, F32) for s in shapes],
        in_specs=[vmem] * len(args),
        out_specs=[vmem] * len(shapes),
        scratch_shapes=[pltpu.VMEM(s, t) for s, t in SCRATCH.values()]
        + [pltpu.SemaphoreType.DMA((240,)), pltpu.SemaphoreType.DMA((260,))],
        compiler_params=pltpu.CompilerParams(
            collective_id=0, has_side_effects=True, vmem_limit_bytes=48 * 1024 * 1024
        ),
    )(*args)
    return tuple(o.reshape(-1) if o.shape[0] == 1 else o for o in outs)


def solution(mesh):
    in_specs = (
        P("user", None), P("item", None), P("user"), P("item"), P("user"), P("item"),
        P("user", "item"), P("item", "user"), P(None, "item"), P(None, "item"), P("item"), P("item"),
        P(None, "user"), P(None, "user"), P("user"), P("user"),
    )
    out_specs = (
        P("user", "item"), P("user", "item"), P("item"), P("item"),
        P("item", "user"), P("item", "user"), P("user"), P("user"),
    )
    return jax.shard_map(on_device, mesh=mesh, in_specs=in_specs, out_specs=out_specs, check_vma=False)
```

time: 1380 us -> 122 us (0.09)
  waiting for transfers between devices: 950 us -> 0 us
  blocking collectives: 382 us -> 0 us
  Pallas kernels: 0 us -> 112 us
  matrix products: 15 us -> 0 us
  between operations: 14.8 us -> 0.82 us
    unnamed x11 -> x0, waiting for transfers between devices: 503 us -> none
    reduce_scatter x4 -> x0, waiting for transfers between devices: 403 us -> none  [the longest x1 223 us: on_device(): lax.psum_scatter(item_terms, 'user', scatter_dimension=1, tiled=True)]
    psum x6 -> x0, blocking collectives: 315 us -> none  [the longest x1 70 us: on_device(): user_total = lax.psum(jnp.sum(user_pre, 0), 'user')]
    pallas_call x0 -> x1, Pallas kernels: none -> 112 us  [on_device(): pl.pallas_call(kernel, out_shape=[jax.ShapeDtypeStruct(s, F32) for s in s...]
    all_gather x1 -> x0, blocking collectives: 66.7 us -> none  [on_device(): lax.all_gather(item_active.astype(jnp.bfloat16), 'user', axis=1, tiled=True)]
    all_gather x3 -> x0, waiting for transfers between devices: 44.1 us -> none  [the longest x1 44.1 us: on_device(): user_whole = lax.all_gather(user_content, 'item', axis=1, tiled=True)]
    dot_general x12 -> x0, matrix products: 15 us -> none  [the longest x5 6.46 us: contract_rows(): lax.dot_general(left, right, (((0,), (0,)), ((), ())), preferred_element_...]
  transfers between devices with their start and end apart: 9 -> 0, of which waited for: 7 -> 0; matrix products, arithmetic and copies ran while one was open for 2% -> 0% of each run, Pallas kernels for 0% -> 0%
where the time goes in v1:
time: 122 us; the launch traced here: 121 us
  Pallas kernels  112 us (92%)
  local copies, waits for them, and re-layouts  8.4 us (7%)
    pallas_call x1, Pallas kernels, on_device(): pl.pallas_call(kernel, out_shape=[jax.ShapeDtypeStruct(s, F32) for s in s...  112 us
    unnamed x39, local copies, waits for them, and re-layouts  8.4 us

profile of v1, /device:TPU:1, one launch (start us, length us, event | category | flops | bytes accessed | tf_op | source)
XLA Modules:
  0.0 121.2 jit_solution(7900392847179460989)
XLA Ops:
  0.6 0.0 copy-start.11
  0.6 0.9 copy.24.ic
  1.6 0.9 copy.25.upw
  2.4 0.0 copy-start.12
  2.5 0.9 copy.27.ipw
  3.3 0.0 copy-done.11
  3.3 0.0 copy-start
  3.3 0.0 copy-start.1
  3.4 0.3 copy.26.ucw
  3.6 0.0 copy-done.12
  3.6 0.0 copy-start.2
  3.7 0.0 copy-start.3
  3.7 0.0 copy-start.4
  3.7 0.0 copy-start.5
  3.7 0.0 copy-start.6
  3.7 0.0 copy-start.7
  3.7 0.0 copy-start.8
  3.7 0.0 copy-start.9
  3.7 0.0 copy-start.10
  3.8 0.3 copy.28.icw
  4.0 0.3 copy-done
  4.4 0.2 copy-done.1
  4.5 0.1 copy-done.2
  4.6 0.0 copy-done.3
  4.6 0.0 copy-done.4
  4.6 0.0 copy-done.5
  4.6 0.0 copy-done.6
  4.6 0.0 copy-done.7
  4.6 0.0 copy-done.8
  4.7 0.0 copy-done.9
  4.7 0.0 copy-done.10
  4.7 112.0 %shard_map.215 = (f32[8,64]{1,0:T(8,128)S(1)}, f32[64,64]{1,0:T(8,128)S(1)}, f32[1,64]{1,0:T(1,128)S(1)}, f32[1,64]{1,0:T(1,128)S(1)}, f32[16,32]{1,0:T(8,128)S(...) custom-call(bf16[1024,256]{1,0:T(8,128)(2,1)S(1)} %copy-done, ...), custom_call_target="tpu_custom_call" | custom-call | tf_op jit(solution)/shard_map/pallas_call | solution.py:644
  116.7 0.7 copy.29
  117.4 0.6 copy.37
  118.0 0.6 copy.38
  118.6 0.5 copy.39
  119.1 0.5 copy.40
  119.6 0.6 copy.41
  120.2 0.5 copy.42
  120.7 0.5 copy.43
Async XLA Ops:
  0.6 2.7 %copy-start.11 = (bf16[2048,64]{0,1:T(8,128)(2,1)S(1)}, bf16[2048,64]{0,1:T(8,128)(2,1)}, u32[]{:S(2)}) copy-start(bf16[2048,64]{0,1:T(8,128)(2,1)} %param.25) | copy-start | bytes 786436
  2.4 1.2 copy-start.12
  3.3 1.1 copy-start
  3.3 1.2 copy-start.1
  3.6 1.0 copy-start.2
  3.7 1.0 copy-start.3
  3.7 1.0 copy-start.4
  3.7 1.0 copy-start.5
  3.7 0.9 copy-start.6
  3.7 0.9 copy-start.7
  3.7 0.9 copy-start.8
  3.7 0.9 copy-start.9
  3.7 0.9 copy-start.10

commit v2 on v1

v2 whole, which is shorter than its diff:
```python
import functools
import math

import jax
import jax.numpy as jnp
from jax import lax
from jax.experimental import pallas as pl
from jax.experimental.pallas import tpu as pltpu
from jax.sharding import PartitionSpec as P

EPSILON = 1e-05
YH, Z, YL, X, C = 4, 8, 2, 4, 2
N_USER, N_ITEM, CHIPS = YH * Z, YL * X * C, YL * X
USERS, ITEMS, HID, RANK, CONTENT = 16384, 4096, 1024, 256, 2048
UB = 256
IB = 256
UH = 128
IH = 32
BF, F32 = jnp.bfloat16, jnp.float32
MESH = pl.DeviceIdType.MESH

NN = (((1,), (0,)), ((), ()))
NT = (((1,), (1,)), ((), ()))
TN = (((0,), (0,)), ((), ()))


def dot(left, right, dims=NN):
    return lax.dot_general(left, right, dims, preferred_element_type=F32)


class Counter:
    def __init__(self):
        self.count = 0

    def take(self, amount=1):
        self.count += amount
        return self.count - amount


def kernel(
    h_ut, h_it, h_uid, h_iid, h_udrop, h_idrop, h_uc, h_ic, h_upw, h_ucw, h_ugain, h_ushift, h_ipw, h_icw, h_igain,
    h_ishift,
    h_o0, h_o1, h_o2, h_o3, h_o4, h_o5, h_o6, h_o7,
    ut, it, uid, iid, udrop, idrop, uc, ugain, ushift, ipw, icw, igain, ishift, o_upw, o_ucw, o_ug, o_us, o_ipw, o_icw, o_ig, o_is, xb, cT, wT, gsd, gss, wT3, ipref, upref, uinp, iinp, su, sz, si, ue, eb, tgt, sig, tbs, sb, tf,
    utf, utb, r1, r2, ys, yr, isd, ir, zs, zr, du, dz8, di, pk, ps, pa, pb, pza, pyb, qa, qb, pya, pzb, gi, gr,
    span, ssem, rsem, lsem,
):
    u, i = lax.axis_index("user"), lax.axis_index("item")
    yh, z = lax.div(u, Z), lax.rem(u, Z)
    yl, x, c = lax.div(i, X * C), lax.rem(lax.div(i, C), X), lax.rem(i, C)
    sent, landed = [0], Counter()
    stores = []

    def at(dyh=0, dz=0, dyl=0, dx=0, dc=0):
        return {
            "user": lax.rem(yh + dyh, YH) * Z + lax.rem(z + dz + Z, Z),
            "item": lax.rem(yl + dyl, YL) * (X * C) + lax.rem(x + dx + X, X) * C + lax.rem(c + dc, C),
        }

    def YHI(d):
        return lax.rem(yh + d + YH, YH)

    def ZI(d):
        return lax.rem(z + d + Z, Z)

    def XI(d):
        return lax.rem(x + d + X, X)

    def CHIP(row, d):
        return lax.rem(yl + row, YL) * X + XI(d)

    def CI(r):
        return lax.rem(c + r, C)

    def lines(ref):
        return math.prod(ref.shape) * (1 if ref.dtype == BF else 2) // 128

    def send(src, dst, device, landing):
        copy = pltpu.make_async_remote_copy(
            src_ref=src, dst_ref=dst, send_sem=ssem.at[len(sent) - 1], recv_sem=rsem.at[landing],
            device_id=device, device_id_type=MESH,
        )
        copy.start()
        sent[-1] += lines(src)

    def recv(dst, landing):
        pltpu.make_async_remote_copy(
            src_ref=dst, dst_ref=dst, send_sem=ssem.at[0], recv_sem=rsem.at[landing],
            device_id=at(dc=1), device_id_type=MESH,
        ).wait_recv()

    def store(source, result):
        copy = pltpu.make_async_copy(source, result, lsem.at[17 + len(stores)])
        copy.start()
        stores.append(copy)

    def recv_all(count, like, landing):
        whole = span.at[pl.ds(0, count * lines(like)), :]
        recv(whole, landing)

    barrier = pltpu.get_barrier_semaphore()
    peers = [dict(dyl=a, dx=b, dc=r) for a in range(YL) for b in range(X) for r in range(C) if a or b or r]
    peers += [dict(dz=d) for d in range(1, Z)]
    peers += [dict(dyh=e, dc=r) for e in range(1, YH) for r in range(C)]
    for peer in peers:
        pl.semaphore_signal(barrier, inc=1, device_id=at(**peer), device_id_type=MESH)

    own = lax.rem(yl, YL) * X + x
    half = pl.ds(pl.multiple_of(c * UB, UB), UB)
    loads = [
        (h_ic, cT.at[yh, z]), (h_uc, uc), (h_uc.at[half, :], xb.at[own, c]),
        (h_ucw, wT.at[c, :, pl.ds(0, CONTENT)]), (h_upw, wT.at[c, :, pl.ds(CONTENT, RANK)]),
        (h_ugain, ugain), (h_ushift, ushift), (h_icw, icw), (h_it, it), (h_iid, iid), (h_idrop, idrop),
        (h_ut, ut), (h_uid, uid), (h_udrop, udrop), (h_ipw, ipw), (h_igain, igain), (h_ishift, ishift),
    ]
    loads = [pltpu.make_async_copy(a, b, lsem.at[k]) for k, (a, b) in enumerate(loads)]
    for load in loads:
        load.start()
    lane = lax.broadcasted_iota(jnp.int32, (1, 128), 1)
    low = lane < 64
    mine_mask = low == (c == 0)

    def twice(v):
        return jnp.concatenate([v, v], axis=1)

    for load in loads[:7]:
        load.wait()
    sub8 = lax.broadcasted_iota(jnp.int32, (8, 128), 0)
    gsd[...] = jnp.where(sub8 == 0, twice(ugain[...]), twice(ushift[...]))

    pl.semaphore_wait(barrier, len(peers))

    n_iy = landed.take(YH)
    n_iz = [[landed.take(YH) for _ in range(Z // 2)] for _ in range(2)]
    n_w, n_gs, n_pref, n_us = landed.take(), landed.take(), landed.take(), landed.take()
    n_uy = landed.take(2)
    n_ux = [[[landed.take(2) for _ in range(2)] for _ in range(2)] for _ in range(2)]

    def item_y(buf):
        for e in range(1, YH):
            send(buf.at[yh, z], buf.at[yh, z], at(dyh=e), n_iy + e)

    def item_z(buf, base, step, e, direction):
        if step < Z // 2 or (e < 2) == (direction == 1):
            k = 0 if direction == 1 else 1
            slot = buf.at[YHI(-e), ZI(-direction * (step - 1))]
            send(slot, slot, at(dz=direction), base[k][step - 1] + e)

    def item_z_wait(buf, base, step, e, direction):
        if step < Z // 2 or (e < 2) == (direction == 1):
            k = 0 if direction == 1 else 1
            recv(buf.at[YHI(-e), ZI(-direction * step)], base[k][step - 1] + e)

    def user_slot(buf, row, d, piece, relative):
        return buf.at[CHIP(row, d), CI(piece) if relative else piece]

    def user_x_forward(buf, base, row, relative):
        for direction, piece in ((1, 0), (-1, 1)):
            k = 0 if direction == 1 else 1
            slot = user_slot(buf, row, -direction, piece, relative)
            recv(slot, base[row][k][0] + piece)
            send(slot, slot, at(dx=direction), base[row][k][1] + piece)

    def user_x_rest(buf, base, row, relative):
        for direction, piece in ((1, 1), (-1, 0)):
            k = 0 if direction == 1 else 1
            recv(user_slot(buf, row, -direction, piece, relative), base[row][k][0] + piece)

    def user_x_far(buf, base, row, relative):
        recv(user_slot(buf, row, 2, 0, relative), base[row][0][1] + 0)
        recv(user_slot(buf, row, 2, 1, relative), base[row][1][1] + 1)

    item_z(cT, n_iz, 1, 0, 1)
    item_z(cT, n_iz, 1, 0, -1)
    for r in range(C):
        half = uc.at[pl.ds(pl.multiple_of(CI(r) * UB, UB), UB), :]
        slot = xb.at[CHIP(0, 0), c]
        for direction in (1, -1):
            send(half, slot, at(dx=direction, dc=r), n_ux[0][0 if direction == 1 else 1][0] + r)
        send(half, slot, at(dyl=1, dc=r), n_uy + r)
        if r:
            send(half, slot, at(dc=1), n_us)
    item_y(cT)
    send(wT.at[c], wT.at[c], at(dc=1), n_w)
    send(gsd, gss, at(dc=1), n_gs)

    for load in loads[7:]:
        load.wait()
    for zz in range(Z):
        wT3[zz] = jnp.concatenate(
            [icw[:, (a * Z + zz) * 64:(a * Z + zz + 1) * 64] for a in range(YH)], axis=1
        )
    for e in range(1, YH):
        recv(cT.at[YHI(-e), z], n_iy + e)
        item_z(cT, n_iz, 1, e, 1)
        item_z(cT, n_iz, 1, e, -1)
    for r in range(C):
        slot = user_slot(xb, 1, 0, r, True)
        recv(slot, n_uy + r)
        for direction in (1, -1):
            send(slot, slot, at(dx=direction), n_ux[1][0 if direction == 1 else 1][0] + r)
    user_x_forward(xb, n_ux, 0, True)

    def column(row):
        return jnp.broadcast_to(row.astype(F32), (128, 256)).T

    def take(table, ids, drop):
        ids, keep = column(ids), 1.0 - column(drop)
        places = lax.broadcasted_iota(jnp.int32, (256, 128), 1).astype(F32)
        one_hot = jnp.concatenate(
            [(ids == places + 128.0 * t).astype(F32).astype(BF) for t in range(8)], axis=1
        )
        chosen = dot(one_hot, table)
        return chosen.astype(BF), (chosen * jnp.concatenate([keep, keep], axis=1)).astype(BF)

    chosen, kept = take(it[...], iid[...], idrop[...])
    ipref[c] = chosen
    iinp[...] = kept
    send(ipref.at[c], ipref.at[c], at(dc=1), n_pref)

    for e in range(YH):
        for direction in (1, -1):
            item_z_wait(cT, n_iz, 1, e, direction)
            item_z(cT, n_iz, 2, e, direction)
    user_x_forward(xb, n_ux, 1, True)

    mine = c == 0
    chosen, kept = take(
        ut[...],
        jnp.where(mine, uid[:, 0:UB], uid[:, UB:]),
        jnp.where(mine, udrop[:, 0:UB], udrop[:, UB:]),
    )
    upref[...] = chosen
    uinp[...] = kept
    recv(wT.at[CI(1)], n_w)
    recv(gss, n_gs)
    gain_shift = jnp.where(mine_mask, gsd[...], gss[...])
    gain, shift = gain_shift[0:1, :], gain_shift[1:2, :]
    preT = dot(ipw[...], iinp[...], NT)

    def user_weights(first):
        lanes = pl.ds(first, 256)
        return jnp.concatenate([wT[0, :, lanes], wT[1, :, lanes]], axis=0)

    pre = dot(uinp[...], user_weights(CONTENT), NT)

    def item_part(zi):
        return dot(wT3[zi], jnp.concatenate([cT[a, zi] for a in range(YH)], axis=0))

    def user_part(chip):
        rows = user_weights(pl.multiple_of(chip * 256, 256))
        return dot(jnp.concatenate([xb[chip, 0], xb[chip, 1]], axis=1), rows, NT)

    for e in range(YH):
        for direction in (1, -1):
            item_z_wait(cT, n_iz, 2, e, direction)
            item_z(cT, n_iz, 3, e, direction)
    preT += item_part(z)
    preT += item_part(ZI(1))
    preT += item_part(ZI(-1))
    recv(user_slot(xb, 0, 0, 1, True), n_us)
    pre += user_part(CHIP(0, 0))
    pre += user_part(CHIP(1, 0))
    user_x_rest(xb, n_ux, 0, True)
    pre += user_part(CHIP(0, 1))
    pre += user_part(CHIP(0, -1))
    user_x_far(xb, n_ux, 0, True)
    pre += user_part(CHIP(0, 2))
    user_x_rest(xb, n_ux, 1, True)
    pre += user_part(CHIP(1, 1))
    pre += user_part(CHIP(1, -1))
    user_x_far(xb, n_ux, 1, True)
    pre += user_part(CHIP(1, 2))

    n_su, n_sz, n_si = landed.take(), landed.take(), landed.take()

    def rows_of(*rows):
        result = jnp.zeros((8, 128), F32)
        for k, row in enumerate(rows):
            result = jnp.where(sub8 == k, row, result)
        return result

    def user_first(buf, base):
        for e in range(YH):
            for r in range(C):
                if e or r:
                    send(buf.at[yh, c], buf.at[yh, c], at(dyh=e, dc=r), base)

    def user_first_wait(buf, base):
        recv_all(YH * C - 1, buf.at[0, 0], base)

    def user_second(buf, base):
        for d in range(1, Z):
            send(buf.at[z], buf.at[z], at(dz=d), base)

    def user_second_wait(buf, base):
        recv_all(Z - 1, buf.at[0], base)

    def item_all(buf, base):
        for a in range(YL):
            for b in range(X):
                for r in range(C):
                    if a or b or r:
                        send(buf.at[i], buf.at[i], at(dyl=a, dx=b, dc=r), base)

    def item_all_wait(buf, base):
        recv_all(N_ITEM - 1, buf.at[0], base)

    def to_rows(first, second):
        both = jnp.where(lane == 0, first, jnp.where(lane == 1, second, 0.0))
        return jnp.concatenate([both, jnp.zeros((96, 128), F32)], axis=0).T[0:8, :]

    def to_columns(rows):
        full = jnp.concatenate([rows, jnp.zeros((120, 128), F32)], axis=0).T
        return full[0:IH, 0:1], full[0:IH, 1:2]

    mean = jnp.sum(pre, 0, keepdims=True) * (1.0 / UB)
    gap = pre - mean
    su[yh, c] = rows_of(mean, jnp.sum(gap * gap, 0, keepdims=True))
    user_first(su, n_su)

    for e in range(YH):
        for direction in (1, -1):
            item_z_wait(cT, n_iz, 3, e, direction)
            item_z(cT, n_iz, 4, e, direction)
    preT += item_part(ZI(2))
    preT += item_part(ZI(-2))
    def combine(means, squares, each):
        total = sum(means[1:], means[0]) * (1.0 / len(means))
        spread = sum(squares[1:], squares[0])
        apart = [(m - total) * (m - total) for m in means]
        return total, spread + float(each) * sum(apart[1:], apart[0])

    user_first_wait(su, n_su)
    blocks = [su[a, r] for a in range(YH) for r in range(C)]
    mean, spread = combine([b[0:1] for b in blocks], [b[1:2] for b in blocks], UB)
    sz[z] = rows_of(mean, spread)
    user_second(sz, n_sz)
    recv(ipref.at[CI(1)], n_pref)
    for r in range(C):
        tgt[r] = dot(upref[...], ipref[r], NT)
    for e in range(YH):
        for direction in (1, -1):
            item_z_wait(cT, n_iz, 4, e, direction)
    preT += item_part(ZI(3))
    preT += item_part(ZI(-3))
    preT += item_part(ZI(4))
    imean = jnp.sum(preT, 1, keepdims=True) * (1.0 / IB)
    gap = preT - imean
    si[i] = to_rows(imean, jnp.sum(gap * gap, 1, keepdims=True))
    item_all(si, n_si)

    item_all_wait(si, n_si)
    blocks = [si[k] for k in range(N_ITEM)]
    imean, ispread = combine([b[0:1] for b in blocks], [b[1:2] for b in blocks], IB)
    imean, iinv = to_columns(rows_of(imean, lax.rsqrt(ispread * (1.0 / ITEMS) + EPSILON)))

    sent.append(0)
    n_ey = landed.take(YH)
    n_ez = [[landed.take(YH) for _ in range(Z // 2)] for _ in range(2)]
    n_es = landed.take()
    n_vy = landed.take(2)
    n_vx = [[[landed.take(2) for _ in range(2)] for _ in range(2)] for _ in range(2)]

    def as_column(row):
        square = jnp.broadcast_to(row, (IH, IH))
        diagonal = lax.broadcasted_iota(jnp.int32, (IH, IH), 0) == lax.broadcasted_iota(jnp.int32, (IH, IH), 1)
        return jnp.sum(jnp.where(diagonal, square, 0.0), 1, keepdims=True)

    igain_c, ishift_c = as_column(igain[...]), as_column(ishift[...])
    inorm = (preT - imean) * iinv
    iact = jnp.tanh(inorm * igain_c + ishift_c)
    ebc = eb.at[c]
    ebc[yh, z] = iact.astype(BF)

    def emb_spread(e):
        slot = ebc.at[YHI(-e), z]
        for k, d in ((0, 1), (1, -1)):
            for hop in (2, 1):
                send(slot, slot, at(dz=d * hop), n_ez[k][hop - 1] + e)

    def emb_forward(e):
        for k, d in ((0, 1), (1, -1)):
            item_z_wait(ebc, n_ez, 2, e, d)
            slot = ebc.at[YHI(-e), ZI(-2 * d)]
            if (e < 2) == (d == 1):
                send(slot, slot, at(dz=2 * d), n_ez[k][3] + e)
            send(slot, slot, at(dz=d), n_ez[k][2] + e)

    for e in range(1, YH):
        send(ebc.at[yh, z], ebc.at[yh, z], at(dyh=e), n_ey + e)
    emb_spread(0)

    user_second_wait(sz, n_sz)
    blocks = [sz[k] for k in range(Z)]
    mean, spread = combine([b[0:1] for b in blocks], [b[1:2] for b in blocks], UB * YH * C)
    inv = lax.rsqrt(spread * (1.0 / USERS) + EPSILON)
    norm = (pre - mean) * inv
    act = jnp.tanh(norm * gain + shift)
    emb = act.astype(BF)
    ue[own, 0] = emb[0:128, :]
    ue[own, 1] = emb[128:256, :]
    for h in range(2):
        for direction in (1, -1):
            send(ue.at[own, h], ue.at[own, h], at(dx=direction), n_vx[0][0 if direction == 1 else 1][0] + h)
        send(ue.at[own, h], ue.at[own, h], at(dyl=1), n_vy + h)

    def share(group):
        send(ebc.at[:, group], ebc.at[:, group], at(dc=1), n_es)

    for e in (1, 3, 2):
        recv(ebc.at[YHI(-e), z], n_ey + e)
        emb_spread(e)
    share(z)
    for h in range(2):
        slot = ue.at[CHIP(1, 0), h]
        recv(slot, n_vy + h)
        for direction in (1, -1):
            send(slot, slot, at(dx=direction), n_vx[1][0 if direction == 1 else 1][0] + h)
    user_x_forward(ue, n_vx, 0, False)
    emb_forward(0)
    user_x_forward(ue, n_vx, 1, False)
    for e in (1, 3, 2):
        emb_forward(e)
    share(ZI(-2))
    share(ZI(2))
    for step in (1, 3):
        for e in range(YH):
            for direction in (1, -1):
                item_z_wait(ebc, n_ez, step, e, direction)
        share(ZI(-step))
        share(ZI(step))
    for row in range(YL):
        user_x_rest(ue, n_vx, row, False)
        user_x_far(ue, n_vx, row, False)
    for e in range(YH):
        for direction in (1, -1):
            item_z_wait(ebc, n_ez, Z // 2, e, direction)
    share(ZI(4))
    recv_all(Z, ebc.at[:, 0], n_es)

    sent.append(0)
    n_sb = landed.take()
    n_r1, n_r2, n_yr = landed.take(2), landed.take(4), landed.take()
    n_ir = [[landed.take(2) for _ in range(Z // 2)] for _ in range(2)]
    n_zr = landed.take()
    n_du, n_d8, n_di = landed.take(), landed.take(), landed.take()
    n_ps, n_pz, n_py, n_p2z, n_p2y, n_gr = (landed.take() for _ in range(6))
    factor = 1.0 / math.sqrt(HID)
    loss_weight = 64.0 / math.sqrt(USERS * ITEMS)

    def user_rows(k):
        return jnp.concatenate([ue[k, 0], ue[k, 1]], axis=0)

    def item_rows(r, k):
        return eb[r, k].reshape(256, IB)

    for r in range(C):
        total = None
        for k in range(4):
            part = dot(jnp.concatenate([user_rows(2 * k), user_rows(2 * k + 1)], axis=1), item_rows(r, k))
            total = part if total is None else total + part
        sig[r] = (loss_weight * (total * factor - tgt[r])).astype(BF)

    def user_term(chip):
        rows = lax.div(chip, 2), lax.rem(chip, 2) * 4
        total = None
        for r in range(C):
            part = dot(sig[r], eb[r, rows[0], pl.ds(rows[1], 4)].reshape(UH, IB), NT)
            total = part if total is None else total + part
        return total * factor

    def put_term(a, d):
        term = user_term(a * X + XI(d)).reshape(2, 128, 128)
        utf[a, XI(d)] = term
        utb[a, XI(d)] = term.astype(BF)

    for a in range(YL):
        put_term(a, 2)
    send(utb.at[:, XI(2), 0], r1.at[0], at(dx=1), n_r1)
    send(utb.at[:, XI(2), 1], r1.at[1], at(dx=-1), n_r1 + 1)
    for a in range(YL):
        put_term(a, 1)
    send(utb.at[:, XI(1), 1], r2.at[0, 1], at(dx=1), n_r2 + 1)
    for a in range(YL):
        put_term(a, -1)
    send(utb.at[:, XI(-1), 0], r2.at[1, 0], at(dx=-1), n_r2 + 2)

    def item_term(signal, k):
        both = jnp.concatenate([user_rows(2 * k), user_rows(2 * k + 1)], axis=1)
        return dot(both, signal, TN) * factor

    other = sig[CI(1)]
    for k in range(YH):
        tbs[k] = item_term(other, k).astype(BF).reshape(Z, IH, IB)
        send(tbs.at[k], sb.at[k], at(dc=1), n_sb)
    for k, d in ((0, 1), (1, -1)):
        recv(r1.at[k], n_r1 + k)
        utb[:, XI(d), k] = (utf[:, XI(d), k] + r1[k].astype(F32)).astype(BF)
        send(utb.at[:, XI(d), k], r2.at[k, k], at(dx=d), n_r2 + 2 * k + k)
    own_signal = sig[c]
    for k in range(YH):
        tf[k] = item_term(own_signal, k).reshape(Z, IH, IB)
    recv_all(YH, sb.at[0], n_sb)
    for k in range(YH):
        tf[k] = tf[k] + sb[k].astype(F32)

    for k, d in ((0, 1), (1, -1)):
        h = k
        isd[k, 0, h] = tf[2 * h:2 * h + 2, ZI(4)].astype(BF)
        send(isd.at[k, 0, h], ir.at[k, 0, h], at(dz=d), n_ir[k][0] + h)
    for k, d in ((0, 1), (1, -1)):
        h = 1 - k
        isd[k, 1, h] = tf[2 * h:2 * h + 2, ZI(3 * d)].astype(BF)
        send(isd.at[k, 1, h], ir.at[k, 1, h], at(dz=d), n_ir[k][1] + h)
    for a in range(YL):
        put_term(a, 0)

    def ring(step, halves):
        for hh in halves:
            for k, d in ((0, 1), (1, -1)):
                h = hh if k == 0 else 1 - hh
                recv(ir.at[k, step - 2, h], n_ir[k][step - 2] + h)
                isd[k, step - 1, h] = (
                    tf[2 * h:2 * h + 2, ZI((5 - step) * d)] + ir[k, step - 2, h].astype(F32)
                ).astype(BF)
                send(isd.at[k, step - 1, h], ir.at[k, step - 1, h], at(dz=d), n_ir[k][step - 1] + h)

    ring(2, (0,))
    for k in range(2):
        for h in range(2):
            recv(r2.at[k, h], n_r2 + 2 * k + h)
    for a in range(YL):
        for h in range(2):
            utf[a, x, h] = utf[a, x, h] + r2[0, h, a].astype(F32) + r2[1, h, a].astype(F32)
    ys[...] = utf[lax.rem(yl + 1, YL), x].astype(BF)
    send(ys, yr, at(dyl=1), n_yr)
    ring(3, (1, 0))
    recv(yr, n_yr)
    demb = (utf[yl, x] + yr[...].astype(F32)).reshape(UB, UH)

    dz = demb * (1.0 - act * act)
    du[yh, c] = rows_of(jnp.sum(dz, 0, keepdims=True), jnp.sum(dz * norm, 0, keepdims=True))
    user_first(du, n_du)
    ring(4, (1, 0))
    user_first_wait(du, n_du)
    dz8[z] = sum([du[a, r] for a in range(YH) for r in range(C)][1:], du[0, 0])
    user_second(dz8, n_d8)
    for h in range(2):
        for k in range(2):
            recv(ir.at[k, 3, h], n_ir[k][3] + h)
        part = tf[2 * h:2 * h + 2, z] + ir[0, 3, h].astype(F32) + ir[1, 3, h].astype(F32)
        tf[2 * h:2 * h + 2, z] = part
        zs[2 * h:2 * h + 2] = part.astype(BF)
    for e in range(1, YH):
        send(zs.at[YHI(e)], zr.at[yh], at(dyh=e), n_zr)
    user_second_wait(dz8, n_d8)
    sums = sum([dz8[k] for k in range(1, Z)], dz8[0])
    s_sum, g_sum = sums[0:1, :], sums[1:2, :]
    for result, row in ((o_us, s_sum), (o_ug, g_sum)):
        result[...] = jnp.where(mine, row[:, 0:64], row[:, 64:128])
    store(o_ug, h_o2)
    store(o_us, h_o3)

    sent.append(0)
    dpre = (
        inv * (dz * gain - gain * s_sum * (1.0 / USERS) - norm * (gain * g_sum * (1.0 / USERS)))
    ).astype(BF)

    def turn(v):
        return pltpu.roll(v, 64, 1)

    pref = dot(uinp[...], dpre, TN)
    pref_turned = turn(pref)
    blank = jnp.zeros((8, 128), F32)
    for k in range(CHIPS):
        block = dot(jnp.concatenate([xb[k, 0], xb[k, 1]], axis=1), dpre, TN)
        for q in range(4):
            uu = 4 * k + q
            place = uu // Z, uu % Z
            first, second = block[64 * q:64 * q + 32], block[64 * q + 32:64 * q + 64]
            pk[0, place[0], place[1]] = jnp.concatenate(
                [jnp.where(low, first, turn(second)), pref[8 * uu:8 * uu + 8], blank], axis=0
            ).astype(BF)
            pk[1, place[0], place[1]] = jnp.concatenate(
                [jnp.where(low, turn(first), second), pref_turned[8 * uu:8 * uu + 8], blank], axis=0
            ).astype(BF)
        if k % 2:
            send(pk.at[CI(1), k // 2], ps.at[k // 2], at(dc=1), n_ps)

    recv_all(YH - 1, zs.at[0], n_zr)
    dembT = tf[yh, z]
    for e in range(1, YH):
        dembT += zr[YHI(-e)].astype(F32)
    idz = dembT * (1.0 - iact * iact)
    di[i] = to_rows(jnp.sum(idz, 1, keepdims=True), jnp.sum(idz * inorm, 1, keepdims=True))
    item_all(di, n_di)

    recv_all(YH, ps.at[0], n_ps)
    total = pk[c].astype(F32) + ps[...].astype(F32)
    pa[...] = total[:, :, 0:16].astype(BF)
    pb[...] = total[:, :, 16:48].astype(BF)
    for e in range(1, YH):
        send(pb.at[YHI(e)], pyb.at[yh], at(dyh=e), n_py)
    for d in range(1, Z):
        send(pa.at[:, ZI(d)], pza.at[z], at(dz=d), n_pz)

    item_all_wait(di, n_di)
    sums = sum([di[k] for k in range(1, N_ITEM)], di[0])
    o_is[...] = sums[0:1, 0:IH]
    o_ig[...] = sums[1:2, 0:IH]
    store(o_ig, h_o6)
    store(o_is, h_o7)
    is_sum, ig_sum = to_columns(sums)
    idpre = (
        iinv * (idz * igain_c - igain_c * is_sum * (1.0 / ITEMS) - inorm * (igain_c * ig_sum * (1.0 / ITEMS)))
    ).astype(BF)
    ipg = dot(idpre, iinp[...])
    ipg = jnp.concatenate([ipg, jnp.zeros((96, RANK), F32)], axis=0).T
    for k in range(N_ITEM):
        block = dot(idpre, cT[k // 4, 2 * (k % 4):2 * (k % 4) + 2].reshape(128, IB), NT)
        gi[k] = jnp.concatenate([block, ipg[16 * k:16 * k + 16]], axis=0).astype(BF)
    for a in range(YL):
        for b in range(X):
            for r in range(C):
                if a or b or r:
                    send(gi.at[CHIP(a, b) * C + CI(r)], gr.at[i], at(dyl=a, dx=b, dc=r), n_gr)

    part_b = pb[yh].astype(F32)
    recv_all(YH - 1, pb.at[0], n_py)
    for e in range(1, YH):
        part_b += pyb[YHI(-e)].astype(F32)
    qb[...] = part_b.astype(BF)
    for d in range(1, Z):
        send(qb.at[ZI(d)], pzb.at[z], at(dz=d), n_p2z)
    part_a = pa[:, z].astype(F32)
    recv_all(Z - 1, pza.at[0], n_pz)
    for d in range(1, Z):
        part_a += pza[ZI(-d)].astype(F32)
    qa[...] = part_a.astype(BF)
    for e in range(1, YH):
        send(qa.at[YHI(e)], pya.at[yh], at(dyh=e), n_p2y)

    total = gi[i].astype(F32)
    recv_all(N_ITEM - 1, gr.at[0], n_gr)
    for a in range(YL):
        for b in range(X):
            for r in range(C):
                if a or b or r:
                    total += gr[CHIP(a, -b) * C + CI(r)].astype(F32)
    o_icw[...] = total[0:IH]
    o_ipw[...] = total[IH:, 0:IH]
    store(o_ipw, h_o4)
    store(o_icw, h_o5)

    total_b = qb[z].astype(F32)
    recv_all(Z - 1, qb.at[0], n_p2z)
    for d in range(1, Z):
        total_b += pzb[ZI(-d)].astype(F32)
    total_a = qa[yh].astype(F32)
    recv_all(YH - 1, qa.at[0], n_p2y)
    for e in range(1, YH):
        total_a += pya[YHI(-e)].astype(F32)
    o_ucw[0:16, :] = total_a[:, 0:64]
    o_ucw[16:32, :] = total_b[0:16, 0:64]
    o_ucw[32:48, :] = total_a[:, 64:128]
    o_ucw[48:64, :] = total_b[0:16, 64:128]
    o_upw[...] = total_b[16:24, 0:64]
    store(o_upw, h_o0)
    store(o_ucw, h_o1)

    for k, amount in enumerate(sent):
        whole = span.at[pl.ds(0, amount), :]
        pltpu.make_async_remote_copy(
            src_ref=whole, dst_ref=whole, send_sem=ssem.at[k], recv_sem=rsem.at[0],
            device_id=at(dc=1), device_id_type=MESH,
        ).wait_send()
    for copy in stores:
        copy.wait()
    kernel.counts = sent, landed.count


def finish(*refs):
    results, outputs, held, sem = refs[0:8], refs[8:16], refs[16:24], refs[24]
    loads = [pltpu.make_async_copy(a, b, sem.at[k]) for k, (a, b) in enumerate(zip(results, held))]
    stores = [pltpu.make_async_copy(a, b, sem.at[8 + k]) for k, (a, b) in enumerate(zip(held, outputs))]
    for load in loads:
        load.start()
    for load, store in zip(loads, stores):
        load.wait()
        store.start()
    for store in stores:
        store.wait()


SCRATCH = dict(
    ut=((1024, RANK), BF), it=((1024, RANK), BF), uid=((1, 512), jnp.int32), iid=((1, IB), jnp.int32),
    udrop=((1, 512), jnp.int32), idrop=((1, IB), jnp.int32), uc=((512, 128), BF), ugain=((1, 64), F32),
    ushift=((1, 64), F32), ipw=((IH, RANK), BF), icw=((IH, CONTENT), BF), igain=((1, IH), F32),
    ishift=((1, IH), F32), o_upw=((8, 64), F32), o_ucw=((64, 64), F32), o_ug=((1, 64), F32), o_us=((1, 64), F32),
    o_ipw=((16, IH), F32), o_icw=((IH, 128), F32), o_ig=((1, IH), F32), o_is=((1, IH), F32),
    xb=((CHIPS, 2, UB, 128), BF), cT=((YH, Z, 64, IB), BF), wT=((C, 64, 2304), BF),
    gsd=((8, 128), F32), gss=((8, 128), F32), wT3=((Z, IH, 256), BF),
    ipref=((2, IB, RANK), BF), upref=((UB, RANK), BF), uinp=((UB, RANK), BF), iinp=((IB, RANK), BF),
    su=((YH, C, 8, 128), F32), sz=((Z, 8, 128), F32), si=((N_ITEM, 8, 128), F32),
    ue=((CHIPS, 2, 128, 128), BF), eb=((2, YH, Z, IH, IB), BF), tgt=((2, UB, IB), F32), sig=((2, UB, IB), BF),
    tbs=((YH, Z, IH, IB), BF), sb=((YH, Z, IH, IB), BF), tf=((YH, Z, IH, IB), F32),
    utf=((YL, X, 2, 128, 128), F32), utb=((YL, X, 2, 128, 128), BF), r1=((2, YL, 128, 128), BF),
    r2=((2, 2, YL, 128, 128), BF), ys=((2, 128, 128), BF), yr=((2, 128, 128), BF),
    isd=((2, 4, 2, 2, IH, IB), BF), ir=((2, 4, 2, 2, IH, IB), BF), zs=((YH, IH, IB), BF), zr=((YH, IH, IB), BF),
    du=((YH, C, 8, 128), F32), dz8=((Z, 8, 128), F32), di=((N_ITEM, 8, 128), F32),
    pk=((2, YH, Z, 48, 128), BF), ps=((YH, Z, 48, 128), BF), pa=((YH, Z, 16, 128), BF), pb=((YH, Z, 32, 128), BF),
    pza=((Z, YH, 16, 128), BF), pyb=((YH, Z, 32, 128), BF), qa=((YH, 16, 128), BF), qb=((Z, 32, 128), BF),
    pya=((YH, 16, 128), BF), pzb=((Z, 32, 128), BF),
    gi=((N_ITEM, 48, 128), BF), gr=((N_ITEM, 48, 128), BF), span=((16384, 128), BF),
)


def on_device(ut, it, uid, iid, udrop, idrop, uc, ic, upw, ucw, ugain, ushift, ipw, icw, igain, ishift):
    def row(v):
        return v.reshape(1, v.shape[0])

    args = (ut, it, row(uid), row(iid), row(udrop), row(idrop), uc, ic.T, upw.T, ucw.T, row(ugain), row(ushift),
            ipw.T, icw.T, row(igain), row(ishift))
    shapes = [(8, 64), (64, 64), (1, 64), (1, 64), (16, 32), (32, 128), (1, 32), (1, 32)]
    shapes = [jax.ShapeDtypeStruct(s, F32) for s in shapes]
    hbm = pl.BlockSpec(memory_space=pltpu.HBM)
    results = pl.pallas_call(
        kernel,
        out_shape=shapes,
        in_specs=[hbm] * len(args),
        out_specs=[hbm] * len(shapes),
        scratch_shapes=[pltpu.VMEM(s, t) for s, t in SCRATCH.values()]
        + [pltpu.SemaphoreType.DMA((6,)), pltpu.SemaphoreType.DMA((160,)), pltpu.SemaphoreType.DMA((25,))],
        compiler_params=pltpu.CompilerParams(
            collective_id=0, has_side_effects=True, vmem_limit_bytes=62 * 1024 * 1024
        ),
    )(*args)
    outs = pl.pallas_call(
        finish,
        out_shape=shapes,
        in_specs=[hbm] * len(shapes),
        out_specs=[hbm] * len(shapes),
        scratch_shapes=[pltpu.VMEM(s.shape, F32) for s in shapes] + [pltpu.SemaphoreType.DMA((2 * len(shapes),))],
        compiler_params=pltpu.CompilerParams(vmem_limit_bytes=62 * 1024 * 1024),
    )(*results)
    outs = [o.reshape(-1) if o.shape[0] == 1 else o for o in outs]
    outs[5] = outs[5].T
    return tuple(outs)


def solution(mesh):
    in_specs = (
        P("user", None), P("item", None), P("user"), P("item"), P("user"), P("item"),
        P("user", "item"), P("item", "user"), P(None, "item"), P(None, "item"), P("item"), P("item"),
        P(None, "user"), P(None, "user"), P("user"), P("user"),
    )
    out_specs = (
        P("user", "item"), P("user", "item"), P("item"), P("item"),
        P("item", "user"), P("item", "user"), P("user"), P("user"),
    )
    return jax.shard_map(on_device, mesh=mesh, in_specs=in_specs, out_specs=out_specs, check_vma=False)
```

time: 122 us -> 100 us (0.82)
  Pallas kernels: 112 us -> 98.8 us
  local copies, waits for them, and re-layouts: 8.4 us -> 0 us
    pallas_call x1 -> x2, Pallas kernels: 112 us -> 98.8 us  [the longest x1 97.3 us: on_device(): pl.pallas_call(kernel, out_shape=shapes, in_specs=[hbm] * len(args), out_...]
    unnamed x39 -> x0, local copies, waits for them, and re-layouts: 8.4 us -> none
where the time goes in v2:
time: 100 us; the launch traced here: 99.5 us
  Pallas kernels  98.8 us (99%)
    pallas_call x1, Pallas kernels, on_device(): pl.pallas_call(kernel, out_shape=shapes, in_specs=[hbm] * len(args), out_...  97.3 us

profile of v2, /device:TPU:1, one launch (start us, length us, event | category | flops | bytes accessed | tf_op | source)
XLA Modules:
  0.0 99.5 jit_solution(13651380610058891246)
XLA Ops:
  0.6 97.3 %shard_map.215 = (f32[8,64]{1,0:T(8,128)}, f32[64,64]{1,0:T(8,128)}, f32[1,64]{1,0:T(1,128)}, f32[1,64]{1,0:T(1,128)}, f32[16,32]{1,0:T(8,128)}, /*index=5*/f32[...) custom-call(bf16[1024,256]{1,0:T(8,128)(2,1)} %h_ut.1, bf16[1024,256]{1,0:T(8,128)(2,1)} %h_it.1, s32[1,512]{1,0:T(1,128)} %bitcast.23, ...), custom_call_target="tpu_custom_call" | custom-call | tf_op jit(solution)/shard_map/pallas_call | solution.py:728
  97.9 1.5 %shard_map.216 = (f32[8,64]{1,0:T(8,128)}, f32[64,64]{1,0:T(8,128)}, f32[1,64]{1,0:T(1,128)}, f32[1,64]{1,0:T(1,128)}, f32[16,32]{1,0:T(8,128)}, /*index=5*/f32[...) custom-call(f32[8,64]{1,0:T(8,128)} %get-tuple-element.24.refs_0_, f32[64,64]{1,0:T(8,128)} %get-tuple-element.25.refs_1_, ...), custom_call_target="tpu_custom_call" | custom-call | tf_op jit(solution)/shard_map/pallas_call | solution.py:739

commit v3 on v2

--- a/solution.py
+++ b/solution.py
@@ -41,8 +41,8 @@
     h_ut, h_it, h_uid, h_iid, h_udrop, h_idrop, h_uc, h_ic, h_upw, h_ucw, h_ugain, h_ushift, h_ipw, h_icw, h_igain,
     h_ishift,
     h_o0, h_o1, h_o2, h_o3, h_o4, h_o5, h_o6, h_o7,
-    ut, it, uid, iid, udrop, idrop, uc, ugain, ushift, ipw, icw, igain, ishift, o_upw, o_ucw, o_ug, o_us, o_ipw, o_icw, o_ig, o_is, xb, cT, wT, gsd, gss, wT3, ipref, upref, uinp, iinp, su, sz, si, ue, eb, tgt, sig, tbs, sb, tf,
-    utf, utb, r1, r2, ys, yr, isd, ir, zs, zr, du, dz8, di, pk, ps, pa, pb, pza, pyb, qa, qb, pya, pzb, gi, gr,
+    ut, it, uid, iid, udrop, idrop, uc, ugain, ushift, ipw, icw, igain, ishift, o_upw, o_ucw, o_ug, o_us, o_ipw, o_icw, o_ig, o_is, xb, cT, wT, gsd, gss, wT3, ipref, upref, uinp, iinp, su, sz, si, ue, ueT, xT, eb, tgt, sig, tbs, sb, tf,
+    utf, utb, r1, r2, yr, isd, ir, zs, zr, du, dz8, di, prefs, pk, ps, pa, pb, pza, pyb, qa, qb, pya, pzb, gi, gr,
     span, ssem, rsem, lsem,
 ):
     u, i = lax.axis_index("user"), lax.axis_index("item")
@@ -132,24 +132,29 @@
 
     n_iy = landed.take(YH)
     n_iz = [[landed.take(YH) for _ in range(Z // 2)] for _ in range(2)]
+    n_bz, n_by = landed.take(), landed.take()
+    main, rest = pl.ds(0, 48), pl.ds(48, 16)
     n_w, n_gs, n_pref, n_us = landed.take(), landed.take(), landed.take(), landed.take()
     n_uy = landed.take(2)
     n_ux = [[[landed.take(2) for _ in range(2)] for _ in range(2)] for _ in range(2)]
 
-    def item_y(buf):
-        for e in range(1, YH):
-            send(buf.at[yh, z], buf.at[yh, z], at(dyh=e), n_iy + e)
-
-    def item_z(buf, base, step, e, direction):
+    def item_z(step, e, direction):
         if step < Z // 2 or (e < 2) == (direction == 1):
             k = 0 if direction == 1 else 1
-            slot = buf.at[YHI(-e), ZI(-direction * (step - 1))]
-            send(slot, slot, at(dz=direction), base[k][step - 1] + e)
-
-    def item_z_wait(buf, base, step, e, direction):
+            slot = cT.at[YHI(-e), ZI(-direction * (step - 1)), main]
+            send(slot, slot, at(dz=direction), n_iz[k][step - 1] + e)
+
+    def item_z_wait(step, e, direction):
         if step < Z // 2 or (e < 2) == (direction == 1):
             k = 0 if direction == 1 else 1
-            recv(buf.at[YHI(-e), ZI(-direction * step)], base[k][step - 1] + e)
+            recv(cT.at[YHI(-e), ZI(-direction * step), main], n_iz[k][step - 1] + e)
+
+    def item_forward(step):
+        for e in (0, 1, 3, 2):
+            for direction in (1, -1):
+                item_z_wait(step, e, direction)
+                if step < Z // 2:
+                    item_z(step + 1, e, direction)
 
     def user_slot(buf, row, d, piece, relative):
         return buf.at[CHIP(row, d), CI(piece) if relative else piece]
@@ -170,8 +175,12 @@
         recv(user_slot(buf, row, 2, 0, relative), base[row][0][1] + 0)
         recv(user_slot(buf, row, 2, 1, relative), base[row][1][1] + 1)
 
-    item_z(cT, n_iz, 1, 0, 1)
-    item_z(cT, n_iz, 1, 0, -1)
+    for e in range(1, YH):
+        send(cT.at[yh, z, main], cT.at[yh, z, main], at(dyh=e), n_iy + e)
+    item_z(1, 0, 1)
+    item_z(1, 0, -1)
+    for d in (4, 3, 5, 2, 6, 1, 7):
+        send(cT.at[yh, z, rest], cT.at[yh, z, rest], at(dz=d), n_bz)
     for r in range(C):
         half = uc.at[pl.ds(pl.multiple_of(CI(r) * UB, UB), UB), :]
         slot = xb.at[CHIP(0, 0), c]
@@ -180,7 +189,6 @@
         send(half, slot, at(dyl=1, dc=r), n_uy + r)
         if r:
             send(half, slot, at(dc=1), n_us)
-    item_y(cT)
     send(wT.at[c], wT.at[c], at(dc=1), n_w)
     send(gsd, gss, at(dc=1), n_gs)
 
@@ -190,16 +198,19 @@
         wT3[zz] = jnp.concatenate(
             [icw[:, (a * Z + zz) * 64:(a * Z + zz + 1) * 64] for a in range(YH)], axis=1
         )
-    for e in range(1, YH):
-        recv(cT.at[YHI(-e), z], n_iy + e)
-        item_z(cT, n_iz, 1, e, 1)
-        item_z(cT, n_iz, 1, e, -1)
+    for e in (1, 3, 2):
+        recv(cT.at[YHI(-e), z, main], n_iy + e)
+        item_z(1, e, 1)
+        item_z(1, e, -1)
     for r in range(C):
         slot = user_slot(xb, 1, 0, r, True)
         recv(slot, n_uy + r)
         for direction in (1, -1):
             send(slot, slot, at(dx=direction), n_ux[1][0 if direction == 1 else 1][0] + r)
     user_x_forward(xb, n_ux, 0, True)
+    recv_all(Z - 1, cT.at[0, 0, rest], n_bz)
+    for e in range(1, YH):
+        send(cT.at[yh, :, rest], cT.at[yh, :, rest], at(dyh=e), n_by)
 
     def column(row):
         return jnp.broadcast_to(row.astype(F32), (128, 256)).T
@@ -218,10 +229,7 @@
     iinp[...] = kept
     send(ipref.at[c], ipref.at[c], at(dc=1), n_pref)
 
-    for e in range(YH):
-        for direction in (1, -1):
-            item_z_wait(cT, n_iz, 1, e, direction)
-            item_z(cT, n_iz, 2, e, direction)
+    item_forward(1)
     user_x_forward(xb, n_ux, 1, True)
 
     mine = c == 0
@@ -251,13 +259,7 @@
         rows = user_weights(pl.multiple_of(chip * 256, 256))
         return dot(jnp.concatenate([xb[chip, 0], xb[chip, 1]], axis=1), rows, NT)
 
-    for e in range(YH):
-        for direction in (1, -1):
-            item_z_wait(cT, n_iz, 2, e, direction)
-            item_z(cT, n_iz, 3, e, direction)
-    preT += item_part(z)
-    preT += item_part(ZI(1))
-    preT += item_part(ZI(-1))
+    item_forward(2)
     recv(user_slot(xb, 0, 0, 1, True), n_us)
     pre += user_part(CHIP(0, 0))
     pre += user_part(CHIP(1, 0))
@@ -319,17 +321,23 @@
     su[yh, c] = rows_of(mean, jnp.sum(gap * gap, 0, keepdims=True))
     user_first(su, n_su)
 
-    for e in range(YH):
-        for direction in (1, -1):
-            item_z_wait(cT, n_iz, 3, e, direction)
-            item_z(cT, n_iz, 4, e, direction)
-    preT += item_part(ZI(2))
-    preT += item_part(ZI(-2))
+    item_forward(3)
+    recv_all(YH - 1, cT.at[0, :, rest], n_by)
+    for d in (0, 1, -1, 2, -2):
+        preT += item_part(ZI(d))
     def combine(means, squares, each):
         total = sum(means[1:], means[0]) * (1.0 / len(means))
         spread = sum(squares[1:], squares[0])
         apart = [(m - total) * (m - total) for m in means]
         return total, spread + float(each) * sum(apart[1:], apart[0])
+
+    item_forward(4)
+    for d in (3, -3, 4):
+        preT += item_part(ZI(d))
+    imean = jnp.sum(preT, 1, keepdims=True) * (1.0 / IB)
+    gap = preT - imean
+    si[i] = to_rows(imean, jnp.sum(gap * gap, 1, keepdims=True))
+    item_all(si, n_si)
 
     user_first_wait(su, n_su)
     blocks = [su[a, r] for a in range(YH) for r in range(C)]
@@ -339,17 +347,9 @@
     recv(ipref.at[CI(1)], n_pref)
     for r in range(C):
         tgt[r] = dot(upref[...], ipref[r], NT)
-    for e in range(YH):
-        for direction in (1, -1):
-            item_z_wait(cT, n_iz, 4, e, direction)
-    preT += item_part(ZI(3))
-    preT += item_part(ZI(-3))
-    preT += item_part(ZI(4))
-    imean = jnp.sum(preT, 1, keepdims=True) * (1.0 / IB)
-    gap = preT - imean
-    si[i] = to_rows(imean, jnp.sum(gap * gap, 1, keepdims=True))
-    item_all(si, n_si)
-
+    for k in range(CHIPS):
+        xT[256 * k:256 * k + 256, :] = jnp.concatenate([xb[k, 0], xb[k, 1]], axis=1).T
+    xT[CONTENT:, :] = uinp[...].T
     item_all_wait(si, n_si)
     blocks = [si[k] for k in range(N_ITEM)]
     imean, ispread = combine([b[0:1] for b in blocks], [b[1:2] for b in blocks], IB)
@@ -379,9 +379,14 @@
             for hop in (2, 1):
                 send(slot, slot, at(dz=d * hop), n_ez[k][hop - 1] + e)
 
+    def emb_wait(hops, e, direction):
+        if hops < Z // 2 or (e < 2) == (direction == 1):
+            k = 0 if direction == 1 else 1
+            recv(ebc.at[YHI(-e), ZI(-direction * hops)], n_ez[k][hops - 1] + e)
+
     def emb_forward(e):
         for k, d in ((0, 1), (1, -1)):
-            item_z_wait(ebc, n_ez, 2, e, d)
+            emb_wait(2, e, d)
             slot = ebc.at[YHI(-e), ZI(-2 * d)]
             if (e < 2) == (d == 1):
                 send(slot, slot, at(dz=2 * d), n_ez[k][3] + e)
@@ -403,6 +408,7 @@
     for h in range(2):
         for direction in (1, -1):
             send(ue.at[own, h], ue.at[own, h], at(dx=direction), n_vx[0][0 if direction == 1 else 1][0] + h)
+            send(ue.at[own, h], ue.at[own, h], at(dyl=1, dx=direction), n_vx[1][0 if direction == 1 else 1][0] + h)
         send(ue.at[own, h], ue.at[own, h], at(dyl=1), n_vy + h)
 
     def share(group):
@@ -412,11 +418,6 @@
         recv(ebc.at[YHI(-e), z], n_ey + e)
         emb_spread(e)
     share(z)
-    for h in range(2):
-        slot = ue.at[CHIP(1, 0), h]
-        recv(slot, n_vy + h)
-        for direction in (1, -1):
-            send(slot, slot, at(dx=direction), n_vx[1][0 if direction == 1 else 1][0] + h)
     user_x_forward(ue, n_vx, 0, False)
     emb_forward(0)
     user_x_forward(ue, n_vx, 1, False)
@@ -427,25 +428,32 @@
     for step in (1, 3):
         for e in range(YH):
             for direction in (1, -1):
-                item_z_wait(ebc, n_ez, step, e, direction)
+                emb_wait(step, e, direction)
         share(ZI(-step))
         share(ZI(step))
+    for h in range(2):
+        recv(ue.at[CHIP(1, 0), h], n_vy + h)
     for row in range(YL):
         user_x_rest(ue, n_vx, row, False)
         user_x_far(ue, n_vx, row, False)
+    for k in range(4):
+        ueT[k] = jnp.concatenate(
+            [jnp.concatenate([ue[2 * k + q, 0], ue[2 * k + q, 1]], axis=0) for q in range(2)], axis=1
+        ).T
     for e in range(YH):
         for direction in (1, -1):
-            item_z_wait(ebc, n_ez, Z // 2, e, direction)
+            emb_wait(Z // 2, e, direction)
     share(ZI(4))
     recv_all(Z, ebc.at[:, 0], n_es)
 
     sent.append(0)
     n_sb = landed.take()
-    n_r1, n_r2, n_yr = landed.take(2), landed.take(4), landed.take()
+    n_r1, n_r2, n_yr = landed.take(2), landed.take(8), landed.take()
     n_ir = [[landed.take(2) for _ in range(Z // 2)] for _ in range(2)]
     n_zr = landed.take()
     n_du, n_d8, n_di = landed.take(), landed.take(), landed.take()
-    n_ps, n_pz, n_py, n_p2z, n_p2y, n_gr = (landed.take() for _ in range(6))
+    n_ps = landed.take(YH)
+    n_pz, n_py, n_p2z, n_p2y, n_gr = (landed.take() for _ in range(5))
     factor = 1.0 / math.sqrt(HID)
     loss_weight = 64.0 / math.sqrt(USERS * ITEMS)
 
@@ -479,28 +487,32 @@
         put_term(a, 2)
     send(utb.at[:, XI(2), 0], r1.at[0], at(dx=1), n_r1)
     send(utb.at[:, XI(2), 1], r1.at[1], at(dx=-1), n_r1 + 1)
+
+    def to_rows_of(k, d, h):
+        for row in range(YL):
+            send(
+                utb.at[lax.rem(yl + row, YL), XI(d), h], r2.at[row, k, h], at(dyl=row, dx=d),
+                n_r2 + row * 4 + k * 2 + h,
+            )
+
+    for k, d in ((0, 1), (1, -1)):
+        for a in range(YL):
+            put_term(a, d)
+        to_rows_of(k, d, 1 - k)
     for a in range(YL):
-        put_term(a, 1)
-    send(utb.at[:, XI(1), 1], r2.at[0, 1], at(dx=1), n_r2 + 1)
-    for a in range(YL):
-        put_term(a, -1)
-    send(utb.at[:, XI(-1), 0], r2.at[1, 0], at(dx=-1), n_r2 + 2)
-
-    def item_term(signal, k):
-        both = jnp.concatenate([user_rows(2 * k), user_rows(2 * k + 1)], axis=1)
-        return dot(both, signal, TN) * factor
-
-    other = sig[CI(1)]
+        put_term(a, 0)
+    send(utb.at[lax.rem(yl + 1, YL), x], yr, at(dyl=1), n_yr)
+
+    both = jnp.concatenate([sig[CI(1)], sig[c]], axis=1)
     for k in range(YH):
-        tbs[k] = item_term(other, k).astype(BF).reshape(Z, IH, IB)
+        term = dot(ueT[k], both) * factor
+        tbs[k] = term[:, 0:IB].astype(BF).reshape(Z, IH, IB)
         send(tbs.at[k], sb.at[k], at(dc=1), n_sb)
+        tf[k] = term[:, IB:].reshape(Z, IH, IB)
     for k, d in ((0, 1), (1, -1)):
         recv(r1.at[k], n_r1 + k)
         utb[:, XI(d), k] = (utf[:, XI(d), k] + r1[k].astype(F32)).astype(BF)
-        send(utb.at[:, XI(d), k], r2.at[k, k], at(dx=d), n_r2 + 2 * k + k)
-    own_signal = sig[c]
-    for k in range(YH):
-        tf[k] = item_term(own_signal, k).reshape(Z, IH, IB)
+        to_rows_of(k, d, k)
     recv_all(YH, sb.at[0], n_sb)
     for k in range(YH):
         tf[k] = tf[k] + sb[k].astype(F32)
@@ -513,8 +525,6 @@
         h = 1 - k
         isd[k, 1, h] = tf[2 * h:2 * h + 2, ZI(3 * d)].astype(BF)
         send(isd.at[k, 1, h], ir.at[k, 1, h], at(dz=d), n_ir[k][1] + h)
-    for a in range(YL):
-        put_term(a, 0)
 
     def ring(step, halves):
         for hh in halves:
@@ -527,21 +537,19 @@
                 send(isd.at[k, step - 1, h], ir.at[k, step - 1, h], at(dz=d), n_ir[k][step - 1] + h)
 
     ring(2, (0,))
-    for k in range(2):
-        for h in range(2):
-            recv(r2.at[k, h], n_r2 + 2 * k + h)
-    for a in range(YL):
-        for h in range(2):
-            utf[a, x, h] = utf[a, x, h] + r2[0, h, a].astype(F32) + r2[1, h, a].astype(F32)
-    ys[...] = utf[lax.rem(yl + 1, YL), x].astype(BF)
-    send(ys, yr, at(dyl=1), n_yr)
-    ring(3, (1, 0))
     recv(yr, n_yr)
-    demb = (utf[yl, x] + yr[...].astype(F32)).reshape(UB, UH)
+    demb = utf[yl, x] + yr[...].astype(F32)
+    for row in range(YL):
+        for k in range(2):
+            for h in range(2):
+                recv(r2.at[row, k, h], n_r2 + row * 4 + k * 2 + h)
+            demb += r2[row, k].astype(F32)
+    demb = demb.reshape(UB, UH)
 
     dz = demb * (1.0 - act * act)
     du[yh, c] = rows_of(jnp.sum(dz, 0, keepdims=True), jnp.sum(dz * norm, 0, keepdims=True))
     user_first(du, n_du)
+    ring(3, (1, 0))
     ring(4, (1, 0))
     user_first_wait(du, n_du)
     dz8[z] = sum([du[a, r] for a in range(YH) for r in range(C)][1:], du[0, 0])
@@ -554,6 +562,14 @@
         zs[2 * h:2 * h + 2] = part.astype(BF)
     for e in range(1, YH):
         send(zs.at[YHI(e)], zr.at[yh], at(dyh=e), n_zr)
+    recv_all(YH - 1, zs.at[0], n_zr)
+    dembT = tf[yh, z]
+    for e in range(1, YH):
+        dembT += zr[YHI(-e)].astype(F32)
+    idz = dembT * (1.0 - iact * iact)
+    di[i] = to_rows(jnp.sum(idz, 1, keepdims=True), jnp.sum(idz * inorm, 1, keepdims=True))
+    item_all(di, n_di)
+
     user_second_wait(dz8, n_d8)
     sums = sum([dz8[k] for k in range(1, Z)], dz8[0])
     s_sum, g_sum = sums[0:1, :], sums[1:2, :]
@@ -570,39 +586,45 @@
     def turn(v):
         return pltpu.roll(v, 64, 1)
 
-    pref = dot(uinp[...], dpre, TN)
-    pref_turned = turn(pref)
+    pref = dot(xT[CONTENT:, :], dpre)
+    prefs[0] = pref
+    prefs[1] = turn(pref)
     blank = jnp.zeros((8, 128), F32)
-    for k in range(CHIPS):
-        block = dot(jnp.concatenate([xb[k, 0], xb[k, 1]], axis=1), dpre, TN)
-        for q in range(4):
-            uu = 4 * k + q
-            place = uu // Z, uu % Z
-            first, second = block[64 * q:64 * q + 32], block[64 * q + 32:64 * q + 64]
-            pk[0, place[0], place[1]] = jnp.concatenate(
-                [jnp.where(low, first, turn(second)), pref[8 * uu:8 * uu + 8], blank], axis=0
-            ).astype(BF)
-            pk[1, place[0], place[1]] = jnp.concatenate(
-                [jnp.where(low, turn(first), second), pref_turned[8 * uu:8 * uu + 8], blank], axis=0
-            ).astype(BF)
-        if k % 2:
-            send(pk.at[CI(1), k // 2], ps.at[k // 2], at(dc=1), n_ps)
-
-    recv_all(YH - 1, zs.at[0], n_zr)
-    dembT = tf[yh, z]
-    for e in range(1, YH):
-        dembT += zr[YHI(-e)].astype(F32)
-    idz = dembT * (1.0 - iact * iact)
-    di[i] = to_rows(jnp.sum(idz, 1, keepdims=True), jnp.sum(idz * inorm, 1, keepdims=True))
-    item_all(di, n_di)
-
-    recv_all(YH, ps.at[0], n_ps)
-    total = pk[c].astype(F32) + ps[...].astype(F32)
-    pa[...] = total[:, :, 0:16].astype(BF)
-    pb[...] = total[:, :, 16:48].astype(BF)
-    for e in range(1, YH):
-        send(pb.at[YHI(e)], pyb.at[yh], at(dyh=e), n_py)
-    for d in range(1, Z):
+
+    def weight_terms(e):
+        group = YHI(e)
+        for k in range(2):
+            block = dot(xT[pl.ds(pl.multiple_of(group * 512 + k * 256, 256), 256), :], dpre)
+            for q in range(4):
+                zz = 4 * k + q
+                rows = pl.ds(pl.multiple_of(group * 64 + zz * 8, 8), 8)
+                first, second = block[64 * q:64 * q + 32], block[64 * q + 32:64 * q + 64]
+                pk[0, group, zz] = jnp.concatenate(
+                    [jnp.where(low, first, turn(second)), prefs[0, rows, :], blank], axis=0
+                ).astype(BF)
+                pk[1, group, zz] = jnp.concatenate(
+                    [jnp.where(low, turn(first), second), prefs[1, rows, :], blank], axis=0
+                ).astype(BF)
+        send(pk.at[CI(1), group], ps.at[group], at(dc=1), n_ps + e)
+
+    def weight_sums(e):
+        group = YHI(e)
+        recv(ps.at[group], n_ps + e)
+        both = pk[c, group].astype(F32) + ps[group].astype(F32)
+        pb[group] = both[:, 16:48].astype(BF)
+        if e:
+            send(pb.at[group], pyb.at[yh], at(dyh=e), n_py)
+        pa[group] = both[:, 0:16].astype(BF)
+
+    weight_terms(2)
+    weight_terms(1)
+    weight_sums(2)
+    weight_terms(3)
+    weight_sums(1)
+    weight_terms(0)
+    weight_sums(3)
+    weight_sums(0)
+    for d in (4, 3, 5, 2, 6, 1, 7):
         send(pa.at[:, ZI(d)], pza.at[z], at(dz=d), n_pz)
 
     item_all_wait(di, n_di)
@@ -677,7 +699,6 @@
         ).wait_send()
     for copy in stores:
         copy.wait()
-    kernel.counts = sent, landed.count
 
 
 def finish(*refs):
@@ -703,16 +724,16 @@
     gsd=((8, 128), F32), gss=((8, 128), F32), wT3=((Z, IH, 256), BF),
     ipref=((2, IB, RANK), BF), upref=((UB, RANK), BF), uinp=((UB, RANK), BF), iinp=((IB, RANK), BF),
     su=((YH, C, 8, 128), F32), sz=((Z, 8, 128), F32), si=((N_ITEM, 8, 128), F32),
-    ue=((CHIPS, 2, 128, 128), BF), eb=((2, YH, Z, IH, IB), BF), tgt=((2, UB, IB), F32), sig=((2, UB, IB), BF),
+    ue=((CHIPS, 2, 128, 128), BF), ueT=((4, 256, UB), BF), xT=((2304, UB), BF), eb=((2, YH, Z, IH, IB), BF), tgt=((2, UB, IB), F32), sig=((2, UB, IB), BF),
     tbs=((YH, Z, IH, IB), BF), sb=((YH, Z, IH, IB), BF), tf=((YH, Z, IH, IB), F32),
     utf=((YL, X, 2, 128, 128), F32), utb=((YL, X, 2, 128, 128), BF), r1=((2, YL, 128, 128), BF),
-    r2=((2, 2, YL, 128, 128), BF), ys=((2, 128, 128), BF), yr=((2, 128, 128), BF),
+    r2=((YL, 2, 2, 128, 128), BF), yr=((2, 128, 128), BF),
     isd=((2, 4, 2, 2, IH, IB), BF), ir=((2, 4, 2, 2, IH, IB), BF), zs=((YH, IH, IB), BF), zr=((YH, IH, IB), BF),
     du=((YH, C, 8, 128), F32), dz8=((Z, 8, 128), F32), di=((N_ITEM, 8, 128), F32),
-    pk=((2, YH, Z, 48, 128), BF), ps=((YH, Z, 48, 128), BF), pa=((YH, Z, 16, 128), BF), pb=((YH, Z, 32, 128), BF),
+    prefs=((2, RANK, 128), F32), pk=((2, YH, Z, 48, 128), BF), ps=((YH, Z, 48, 128), BF), pa=((YH, Z, 16, 128), BF), pb=((YH, Z, 32, 128), BF),
     pza=((Z, YH, 16, 128), BF), pyb=((YH, Z, 32, 128), BF), qa=((YH, 16, 128), BF), qb=((Z, 32, 128), BF),
     pya=((YH, 16, 128), BF), pzb=((Z, 32, 128), BF),
-    gi=((N_ITEM, 48, 128), BF), gr=((N_ITEM, 48, 128), BF), span=((16384, 128), BF),
+    gi=((N_ITEM, 48, 128), BF), gr=((N_ITEM, 48, 128), BF), span=((10240, 128), BF),
 )
 
 
@@ -731,7 +752,7 @@
         in_specs=[hbm] * len(args),
         out_specs=[hbm] * len(shapes),
         scratch_shapes=[pltpu.VMEM(s, t) for s, t in SCRATCH.values()]
-        + [pltpu.SemaphoreType.DMA((6,)), pltpu.SemaphoreType.DMA((160,)), pltpu.SemaphoreType.DMA((25,))],
+        + [pltpu.SemaphoreType.DMA((4,)), pltpu.SemaphoreType.DMA((159,)), pltpu.SemaphoreType.DMA((25,))],
         compiler_params=pltpu.CompilerParams(
             collective_id=0, has_side_effects=True, vmem_limit_bytes=62 * 1024 * 1024
         ),

time: 100 us -> 95.1 us (0.951)
  Pallas kernels: 98.8 us -> 94.2 us
    pallas_call x1, Pallas kernels: 97.3 us -> 92.7 us  [on_device(): pl.pallas_call(kernel, out_shape=shapes, in_specs=[hbm] * len(args), out_...]
where the time goes in v3:
time: 95.1 us; the launch traced here: 94.9 us
  Pallas kernels  94.2 us (99%)
    pallas_call x1, Pallas kernels, on_device(): pl.pallas_call(kernel, out_shape=shapes, in_specs=[hbm] * len(args), out_...  92.7 us

profile of v3, /device:TPU:1, one launch (start us, length us, event | category | flops | bytes accessed | tf_op | source)
XLA Modules:
  0.0 94.9 jit_solution(170488706803453445)
XLA Ops:
  0.6 92.7 %shard_map.215 = (f32[8,64]{1,0:T(8,128)}, f32[64,64]{1,0:T(8,128)}, f32[1,64]{1,0:T(1,128)}, f32[1,64]{1,0:T(1,128)}, f32[16,32]{1,0:T(8,128)}, /*index=5*/f32[...) custom-call(bf16[1024,256]{1,0:T(8,128)(2,1)} %h_ut.1, bf16[1024,256]{1,0:T(8,128)(2,1)} %h_it.1, s32[1,512]{1,0:T(1,128)} %bitcast.23, ...), custom_call_target="tpu_custom_call" | custom-call | tf_op jit(solution)/shard_map/pallas_call | solution.py:749
  93.4 1.5 %shard_map.216 = (f32[8,64]{1,0:T(8,128)}, f32[64,64]{1,0:T(8,128)}, f32[1,64]{1,0:T(1,128)}, f32[1,64]{1,0:T(1,128)}, f32[16,32]{1,0:T(8,128)}, /*index=5*/f32[...) custom-call(f32[8,64]{1,0:T(8,128)} %get-tuple-element.24.refs_0_, f32[64,64]{1,0:T(8,128)} %get-tuple-element.25.refs_1_, ...), custom_call_target="tpu_custom_call" | custom-call | tf_op jit(solution)/shard_map/pallas_call | solution.py:760

commit v4 on v3

--- a/solution.py
+++ b/solution.py
@@ -562,14 +562,6 @@
         zs[2 * h:2 * h + 2] = part.astype(BF)
     for e in range(1, YH):
         send(zs.at[YHI(e)], zr.at[yh], at(dyh=e), n_zr)
-    recv_all(YH - 1, zs.at[0], n_zr)
-    dembT = tf[yh, z]
-    for e in range(1, YH):
-        dembT += zr[YHI(-e)].astype(F32)
-    idz = dembT * (1.0 - iact * iact)
-    di[i] = to_rows(jnp.sum(idz, 1, keepdims=True), jnp.sum(idz * inorm, 1, keepdims=True))
-    item_all(di, n_di)
-
     user_second_wait(dz8, n_d8)
     sums = sum([dz8[k] for k in range(1, Z)], dz8[0])
     s_sum, g_sum = sums[0:1, :], sums[1:2, :]
@@ -619,6 +611,14 @@
     weight_terms(2)
     weight_terms(1)
     weight_sums(2)
+    recv_all(YH - 1, zs.at[0], n_zr)
+    dembT = tf[yh, z]
+    for e in range(1, YH):
+        dembT += zr[YHI(-e)].astype(F32)
+    idz = dembT * (1.0 - iact * iact)
+    di[i] = to_rows(jnp.sum(idz, 1, keepdims=True), jnp.sum(idz * inorm, 1, keepdims=True))
+    item_all(di, n_di)
+
     weight_terms(3)
     weight_sums(1)
     weight_terms(0)

time: 95.1 us -> 93.8 us (0.986)
  Pallas kernels: 94.2 us -> 92.9 us
    pallas_call x1, Pallas kernels: 92.7 us -> 91.4 us  [on_device(): pl.pallas_call(kernel, out_shape=shapes, in_specs=[hbm] * len(args), out_...]
where the time goes in v4:
time: 93.8 us; the launch traced here: 93.6 us
  Pallas kernels  92.9 us (99%)
    pallas_call x1, Pallas kernels, on_device(): pl.pallas_call(kernel, out_shape=shapes, in_specs=[hbm] * len(args), out_...  91.4 us

profile of v4, /device:TPU:1, one launch (start us, length us, event | category | flops | bytes accessed | tf_op | source)
XLA Modules:
  0.0 93.6 jit_solution(17741876594609817738)
XLA Ops:
  0.6 91.4 %shard_map.215 = (f32[8,64]{1,0:T(8,128)}, f32[64,64]{1,0:T(8,128)}, f32[1,64]{1,0:T(1,128)}, f32[1,64]{1,0:T(1,128)}, f32[16,32]{1,0:T(8,128)}, /*index=5*/f32[...) custom-call(bf16[1024,256]{1,0:T(8,128)(2,1)} %h_ut.1, bf16[1024,256]{1,0:T(8,128)(2,1)} %h_it.1, s32[1,512]{1,0:T(1,128)} %bitcast.23, ...), custom_call_target="tpu_custom_call" | custom-call | tf_op jit(solution)/shard_map/pallas_call | solution.py:749
  92.0 1.5 %shard_map.216 = (f32[8,64]{1,0:T(8,128)}, f32[64,64]{1,0:T(8,128)}, f32[1,64]{1,0:T(1,128)}, f32[1,64]{1,0:T(1,128)}, f32[16,32]{1,0:T(8,128)}, /*index=5*/f32[...) custom-call(f32[8,64]{1,0:T(8,128)} %get-tuple-element.24.refs_0_, f32[64,64]{1,0:T(8,128)} %get-tuple-element.25.refs_1_, ...), custom_call_target="tpu_custom_call" | custom-call | tf_op jit(solution)/shard_map/pallas_call | solution.py:760
